TPU v7x, 32 devices: a whole 2x2x4 slice. The times are simulated.
32 devices in a mesh: ctx: 16 (over z, y, core), ch: 2 (over x).
Axes of the slice: x: 2, y: 2, z: 4, core: 2. Of those that a mesh axis runs over, the one named last changes fastest.
Arguments:
- mr_query: bfloat16 [4096, 4096], P('ch', 'ctx'), may hold values from -6 to 6
- mr_key: bfloat16 [4096, 4096], P('ch', 'ctx'), may hold values from -6 to 6
- mr_value: bfloat16 [4096, 4096], P('ch', 'ctx'), may hold values from -6 to 6
- mr_filter: float32 [4096, 128], P('ch'), may hold values from -0.5 to 0.5
- proj_weight: bfloat16 [4096, 4096], P('ch'), may hold values from -0.09375 to 0.09375
- li_query: bfloat16 [4096, 4096], P('ch', 'ctx'), may hold values from -6 to 6
- li_key: bfloat16 [4096, 4096], P('ch', 'ctx'), may hold values from -6 to 6
- li_filter: bfloat16 [4096, 4096], P('ch', 'ctx'), may hold values from -0.09375 to 0.09375
- li_skip: float32 [4096], P('ch'), may hold values from 0.5 to 1.5
Outputs:
- gated_out: bfloat16 [4096, 4096], P('ch', 'ctx')
All inputs are finite; a program needn't handle non-finite values.
Results may differ from a plain program's by a relative error of at most 0.0066.
Values may be sent and summed in bfloat16 or wider, within the bound.
No kernel may reach another device: no remote copies, remote signals or barrier semaphores. Data moves between devices by JAX's collectives and lax.ppermute only.
A program may use at most 128 MiB of HBM per device.

v0:
```python
import functools
import math

import jax
import jax.numpy as jnp
import numpy as np
from jax import lax
from jax.experimental import pallas as pl
from jax.experimental.pallas import tpu as pltpu
from jax.sharding import PartitionSpec as P

F32 = jnp.float32
BF16 = jnp.bfloat16
MIB = 1 << 20


def split_table(table):
    high = table.astype(np.float32).astype(BF16)
    low = (table - high.astype(np.float64)).astype(np.float32).astype(BF16)
    return np.asarray(high), np.asarray(low)


def split_value(value):
    high = value.astype(BF16)
    return high, (value - high.astype(F32)).astype(BF16)


def dot(left, right):
    return jnp.dot(left, right, preferred_element_type=F32)


def short_tables(size):
    half = size // 2
    time = np.arange(size)[:, None]
    freq = np.arange(half)[None, :]
    angle = 2.0 * np.pi * (time * freq % size) / size
    forward = np.concatenate([np.cos(angle), -np.sin(angle)], axis=1)
    forward[:, half] = np.where(np.arange(size) % 2 == 0, 1.0, -1.0)
    inverse = forward.T * (2.0 / size)
    inverse[0] /= 2.0
    inverse[half] /= 2.0
    return split_table(forward) + split_table(inverse[:, half:])


def short_filter(window, taps, query, fwd_hi, fwd_lo, inv_hi, inv_lo):
    half = taps.shape[1]
    spec = dot(window, fwd_hi) + dot(window, fwd_lo)
    taps_hi, taps_lo = split_value(taps)
    resp = dot(taps_hi, fwd_hi[:half]) + dot(taps_lo, fwd_hi[:half]) + dot(taps_hi, fwd_lo[:half])
    first = lax.broadcasted_iota(jnp.int32, (taps.shape[0], half), 1) == 0
    resp_re, resp_im = resp[:, :half], resp[:, half:]
    cross = jnp.where(first, 0.0, resp_im)
    own = jnp.where(first, resp_im, resp_re)
    spec_re, spec_im = spec[:, :half], spec[:, half:]
    prod = jnp.concatenate(
        [spec_re * resp_re - spec_im * cross, spec_re * cross + spec_im * own], axis=1
    )
    prod_hi, prod_lo = split_value(prod)
    mixed = dot(prod_hi, inv_hi) + dot(prod_lo, inv_hi) + dot(prod_hi, inv_lo)
    return (query.astype(F32) * mixed).astype(BF16)


def gate_input(key, value):
    return (key.astype(F32) * value.astype(F32)).astype(BF16)


def late_kernel(key, value, query, taps, fwd_hi, fwd_lo, inv_hi, inv_lo, out):
    window = gate_input(key[...], value[...])
    out[...] = short_filter(
        window, taps[...], query[...], fwd_hi[...], fwd_lo[...], inv_hi[...], inv_lo[...]
    )


def early_kernel(border, key, value, query, taps, fwd_hi, fwd_lo, inv_hi, inv_lo, out):
    window = jnp.concatenate([border[...], gate_input(key[...], value[...])], axis=1)
    out[...] = short_filter(
        window, taps[...], query[...], fwd_hi[...], fwd_lo[...], inv_hi[...], inv_lo[...]
    )


def whole_spec(array):
    return pl.BlockSpec(array.shape, lambda *_: (0,) * array.ndim)


def short_conv(border, key, value, query, taps, tables):
    rows, tokens = key.shape
    half = tokens // 2
    block = min(rows, 512)
    table_specs = [whole_spec(t) for t in tables]
    full = pl.BlockSpec((block, tokens), lambda i: (i, 0))
    left = pl.BlockSpec((block, half), lambda i: (i, 0))
    right = pl.BlockSpec((block, half), lambda i: (i, 1))
    if border is None:
        body, specs, args = late_kernel, [full, full, right, left], (key, value, query, taps)
    else:
        body, specs = early_kernel, [left, left, left, left, left]
        args = (border, key, value, query, taps)
    return pl.pallas_call(
        body,
        grid=(rows // block,),
        in_specs=specs + table_specs,
        out_specs=left,
        out_shape=jax.ShapeDtypeStruct((rows, half), BF16),
        compiler_params=pltpu.CompilerParams(vmem_limit_bytes=32 * MIB),
        cost_estimate=pl.CostEstimate(
            flops=10 * rows * tokens * tokens, bytes_accessed=8 * rows * tokens, transcendentals=0
        ),
    )(*args, *tables)


def own_kernel(which, weight, late, early, out):
    del which
    out[...] = dot(weight[...], jnp.concatenate([early[...], late[...]], axis=1))


def other_kernel(which, weight, late, early, total, key, out):
    del which
    values = total[...] + dot(weight[...], jnp.concatenate([early[...], late[...]], axis=1))
    out[...] = (key[...].astype(F32) * values).astype(BF16)


def project(which, weight, late, early, total=None, key=None):
    rows, depth = weight.shape[0], late.shape[0]
    half = late.shape[1]
    block = min(rows, 256)
    moving = pl.BlockSpec((block, 2 * half), lambda i, w: (i, 0))
    specs = [
        pl.BlockSpec((block, depth), lambda i, w: (i, w[0])),
        pl.BlockSpec((depth, half), lambda i, w: (0, 0)),
        pl.BlockSpec((depth, half), lambda i, w: (0, 0)),
    ]
    args = [weight, late, early]
    if total is None:
        body, dtype = own_kernel, F32
    else:
        body, dtype = other_kernel, BF16
        specs += [moving, moving]
        args += [total, key]
    return pl.pallas_call(
        body,
        grid_spec=pltpu.PrefetchScalarGridSpec(
            num_scalar_prefetch=1, grid=(rows // block,), in_specs=specs, out_specs=moving
        ),
        out_shape=jax.ShapeDtypeStruct((rows, 2 * half), dtype),
        compiler_params=pltpu.CompilerParams(vmem_limit_bytes=32 * MIB),
        cost_estimate=pl.CostEstimate(
            flops=4 * rows * depth * half, bytes_accessed=2 * rows * depth, transcendentals=0
        ),
    )(which, *args)


def turn(value, num, den):
    num %= den
    if num < 0:
        num += den
    re, im = value
    if num == 0:
        return value
    if 4 * num == den:
        return (im, -re)
    if 2 * num == den:
        return (-re, -im)
    if 4 * num == 3 * den:
        return (-im, re)
    cos = math.cos(2.0 * math.pi * num / den)
    sin = math.sin(2.0 * math.pi * num / den)
    if 8 * num % den == 0:
        size = math.sqrt(0.5)
        cos, sin = (1 if cos > 0 else -1), (1 if sin > 0 else -1)
        first = re + im if cos == sin else re - im
        second = im - re if cos == sin else im + re
        if cos > 0:
            return (size * first, size * second)
        return ((-size) * first, (-size) * second)
    return (cos * re + sin * im, cos * im - sin * re)


def add(a, b):
    return (a[0] + b[0], a[1] + b[1])


def sub(a, b):
    return (a[0] - b[0], a[1] - b[1])


def dft(values, sign):
    size = len(values)
    if size == 1:
        return values
    half = size // 2
    even = dft([add(values[n], values[n + half]) for n in range(half)], sign)
    odd = dft(
        [turn(sub(values[n], values[n + half]), sign * n, size) for n in range(half)], sign
    )
    out = []
    for n in range(half):
        out += [even[n], odd[n]]
    return out


def odd_part(values, size):
    half = len(values) // 2
    shaped = [turn((values[n], -values[n + half]), n, size) for n in range(half)]
    found = {}
    for r, value in enumerate(dft(shaped, 1)):
        k = 4 * r + 1
        if k < size // 2:
            found[k] = value
        else:
            found[size - k] = (value[0], -value[1])
    return found


def real_dft(values):
    size = len(values)
    if size == 2:
        return {0: (values[0] + values[1], None), 1: (values[0] - values[1], None)}
    half = size // 2
    found = {
        2 * k: v
        for k, v in real_dft([values[n] + values[n + half] for n in range(half)]).items()
    }
    found.update(odd_part([values[n] - values[n + half] for n in range(half)], size))
    return found


def padded_dft(values):
    found = {2 * k: v for k, v in real_dft(values).items()}
    found.update(odd_part(values, 2 * len(values)))
    return found


def odd_back(found, size):
    quarter = size // 4
    terms = []
    for r in range(quarter):
        k = 4 * r + 1
        if k < size // 2:
            terms.append(found[k])
        else:
            value = found[size - k]
            terms.append((value[0], -value[1]))
    back = [turn(value, -n, size) for n, value in enumerate(dft(terms, -1))]
    return [v[0] for v in back] + [-v[1] for v in back]


def real_back(found, size):
    if size == 2:
        return [found[0][0] + found[1][0], found[0][0] - found[1][0]]
    half = size // 2
    even = real_back({k // 2: v for k, v in found.items() if k % 2 == 0}, half)
    odd = odd_back(found, size)
    return [even[n] + odd[n] for n in range(half)] + [even[n] - odd[n] for n in range(half)]


def padded_back(found, size):
    even = real_back({k // 2: v for k, v in found.items() if k % 2 == 0}, size)
    odd = odd_back(found, 2 * size)
    return [e + o for e, o in zip(even, odd)]


def long_tables(slabs, tokens):
    full = 2 * slabs * tokens
    token = np.arange(tokens)
    angle = 2.0 * np.pi * (np.arange(slabs + 1)[:, None] * token[None, :] % full) / full
    cos, sin = np.cos(angle), -np.sin(angle)
    back_scale = np.full((slabs + 1, 1), 2.0 / full)
    back_scale[0] = back_scale[slabs] = 1.0 / full
    inner = 2.0 * np.pi * (token[:, None] * token[None, :] % tokens) / tokens
    re, im = np.cos(inner), -np.sin(inner)
    forward = np.block([[re, im], [-im, re]])
    inverse = np.block([[re, -im], [im, re]])
    turns = [t.astype(np.float32) for t in (cos, sin, cos * back_scale, -sin * back_scale)]
    return turns, split_table(forward), split_table(inverse)


LANES = 128
SUBS = 16


def forward_slabs(source, turn_re, turn_im, high, low):
    slabs, rows, tokens = source.shape
    lanes = min(tokens, LANES)
    subs = min(rows, SUBS)
    for lane in range(0, tokens, lanes):

        def tile(step, carry, lane=lane):
            at = pl.ds(pl.multiple_of(step * subs, subs), subs)
            values = [source[j, at, lane : lane + lanes].astype(F32) for j in range(slabs)]
            for k, (re, im) in padded_dft(values).items():
                cos = turn_re[k : k + 1, lane : lane + lanes]
                sin = turn_im[k : k + 1, lane : lane + lanes]
                if im is None:
                    out = (re * cos, re * sin)
                else:
                    out = (re * cos - im * sin, re * sin + im * cos)
                for part, value in enumerate(out):
                    where = slice(part * tokens + lane, part * tokens + lane + lanes)
                    hi, lo = split_value(value)
                    high[k, at, where] = hi
                    low[k, at, where] = lo
            return carry

        lax.fori_loop(0, rows // subs, tile, 0)


def product3(high, low, table_hi, table_lo):
    a, b = high[...], low[...]
    shape = a.shape
    a = a.reshape(shape[0] * shape[1], shape[2])
    b = b.reshape(shape[0] * shape[1], shape[2])
    out = dot(a, table_hi[...]) + dot(b, table_hi[...]) + dot(a, table_lo[...])
    return out.reshape(shape[0], shape[1], -1)


def response_kernel(source, turn_re, turn_im, table_hi, table_lo, out, high, low):
    forward_slabs(source, turn_re, turn_im, high, low)
    out[...] = product3(high, low, table_hi, table_lo)


def convolve_kernel(
    source, response, turn_re, turn_im, back_re, back_im, fwd_hi, fwd_lo, inv_hi, inv_lo, out, high, low, spec
):
    slabs, rows, tokens = source.shape
    lanes = min(tokens, LANES)
    subs = min(rows, SUBS)
    forward_slabs(source, turn_re, turn_im, high, low)
    spec[...] = product3(high, low, fwd_hi, fwd_lo)

    def multiply(k, carry):
        sig_re, sig_im = spec[k, :, :tokens], spec[k, :, tokens:]
        res_re, res_im = response[k, :, :tokens], response[k, :, tokens:]
        for part, value in enumerate(
            (sig_re * res_re - sig_im * res_im, sig_re * res_im + sig_im * res_re)
        ):
            hi, lo = split_value(value)
            high[k, :, part * tokens : (part + 1) * tokens] = hi
            low[k, :, part * tokens : (part + 1) * tokens] = lo
        return carry

    lax.fori_loop(0, slabs + 1, multiply, 0)
    spec[...] = product3(high, low, inv_hi, inv_lo)
    for lane in range(0, tokens, lanes):

        def tile(step, carry, lane=lane):
            at = pl.ds(pl.multiple_of(step * subs, subs), subs)
            found = {}
            for k in range(slabs + 1):
                re = spec[k, at, lane : lane + lanes]
                im = spec[k, at, tokens + lane : tokens + lane + lanes]
                cos = back_re[k : k + 1, lane : lane + lanes]
                sin = back_im[k : k + 1, lane : lane + lanes]
                if k in (0, slabs):
                    found[k] = (re * cos - im * sin, None)
                else:
                    found[k] = (re * cos - im * sin, re * sin + im * cos)
            for j, value in enumerate(padded_back(found, slabs)):
                out[j, at, lane : lane + lanes] = value.astype(BF16)
            return carry

        lax.fori_loop(0, rows // subs, tile, 0)


def long_call(source, response, tables, start=0, count=None):
    slabs, rows, tokens = source.shape
    block = min(rows, 32)
    turns, forward, inverse = tables
    if response is None:
        body, given = response_kernel, [*turns[:2], *forward]
    else:
        body, given = convolve_kernel, [*turns, *forward, *inverse]
    data = pl.BlockSpec((slabs, block, tokens), lambda i: (0, i, 0))
    wide = pl.BlockSpec((slabs + 1, block, 2 * tokens), lambda i: (0, i, 0))
    scratch = [pltpu.VMEM((slabs + 1, block, 2 * tokens), t) for t in (BF16, BF16, F32)]
    flops = 12 * (slabs + 1) * rows * 4 * tokens * tokens
    if response is None:
        out_spec, out_shape, scratch = wide, ((slabs + 1, rows, 2 * tokens), F32), scratch[:2]
        args, specs = [source], [data]
    else:
        out_spec, out_shape = data, ((slabs, rows, tokens), BF16)
        args, specs = [source, response], [data, wide]
    return pl.pallas_call(
        body,
        grid=(rows // block,),
        in_specs=specs + [whole_spec(t) for t in given],
        out_specs=out_spec,
        out_shape=jax.ShapeDtypeStruct(*out_shape),
        scratch_shapes=scratch,
        compiler_params=pltpu.CompilerParams(vmem_limit_bytes=48 * MIB),
        cost_estimate=pl.CostEstimate(
            flops=flops, bytes_accessed=8 * (slabs + 1) * rows * tokens, transcendentals=0
        ),
    )(*args, *given)


def exchange(value, groups):
    rows, tokens = value.shape
    return lax.all_to_all(
        value.reshape(groups, rows // groups, tokens), "ctx", split_axis=0, concat_axis=0, tiled=True
    )


def on_device(
    mr_query, mr_key, mr_value, mr_filter, proj_weight, li_query, li_key, li_filter, li_skip
):
    rows, tokens = mr_key.shape
    half = tokens // 2
    groups = lax.axis_size("ctx")
    short = short_tables(tokens)
    tables = long_tables(groups, tokens)
    swap = [(0, 1), (1, 0)]

    border = gate_input(mr_key[:, half:], mr_value[:, half:])
    border = lax.ppermute(border, "ctx", [(i, i + 1) for i in range(groups - 1)])
    filter_part = exchange(li_filter, groups)

    late = short_conv(None, mr_key, mr_value, mr_query, mr_filter, short)
    other_late = lax.ppermute(late, "ch", swap)
    early = short_conv(border, mr_key, mr_value, mr_query, mr_filter, short)
    other_early = lax.ppermute(early, "ch", swap)

    me = lax.axis_index("ch").astype(jnp.int32).reshape(1)
    total = project(me, proj_weight, late, early)
    li_input = project(1 - me, proj_weight, other_late, other_early, total, li_key)

    response = long_call(filter_part, None, tables)
    long_part = long_call(exchange(li_input, groups), response, tables)
    long_local = exchange(long_part.reshape(rows, tokens), groups).reshape(rows, tokens)
    gated_out = li_query.astype(F32) * (
        long_local.astype(F32) + li_skip[:, None] * li_input.astype(F32)
    )
    return gated_out.astype(BF16)


def solution(mesh):
    in_specs = (
        P("ch", "ctx"),
        P("ch", "ctx"),
        P("ch", "ctx"),
        P("ch", None),
        P("ch", None),
        P("ch", "ctx"),
        P("ch", "ctx"),
        P("ch", "ctx"),
        P("ch"),
    )
    return jax.shard_map(
        on_device, mesh=mesh, in_specs=in_specs, out_specs=P("ch", "ctx"), check_vma=False
    )
```

profile of v0, /device:TPU:1, one launch (start us, length us, event | category | flops | bytes accessed | tf_op | source)
XLA Modules:
  0.0 145.7 jit_solution(17295530324472198329)
XLA Ops:
  0.0 0.0 copy-start.8
  0.0 0.0 copy-start.9
  0.0 0.0 copy-start.10
  0.1 7.6 %all-to-all-start.1 = ((bf16[16,128,256]{2,1,0:T(8,128)(2,1)}), bf16[16,128,256]{2,1,0:T(8,128)(2,1)}, u32[]{:S(2)}, u32[]{:S(2)}) async-start(bf16[16,128,256]{2,1,0:T(8,128)(2,1)} %bitcast.6), calls=%async_computation.1 | async-start | bytes 2097152 | tf_op jit(solution)/shard_map/all_to_all | solution.py:398
  7.7 0.1 multiply_convert_fusion
  7.8 3.5 %collective-permute-start.1 = (bf16[2048,128]{1,0:T(8,128)(2,1)S(1)}, bf16[2048,128]{1,0:T(8,128)(2,1)S(1)}, u32[]{:S(2)}, u32[]{:S(2)}) collective-permute-start(bf16[2048,128]{1,0:T(8,128)(2,1)S(1)} %multiply_convert_fusion), channel_id=1, source_target_pairs={{0,2},{2,4},{4,6},{6,8},{8,10},{10,12},{12,14},{14,16},{16,18},{18... | collective-permute-start | bytes 1572872 | tf_op jit(solution)/shard_map/ppermute | solution.py:414
  11.5 1.2 copy-done.5
  12.7 5.2 %shard_map.199.late = bf16[2048,128]{1,0:T(8,128)(2,1)} custom-call(bf16[2048,256]{1,0:T(8,128)(2,1)S(1)} %copy-done.2, bf16[2048,256]{1,0:T(8,128)(2,1)S(1)} %copy-done.3, bf16[2048,256]{1,0:T(8,128)(2,1)S(1)} %copy-done.4, f32[2048,128]{1,0:T(8,128)S(1)} %copy-done.5, bf16[256,256]{1,0:T(8,128)(2,1)S(1)} %copy-done.8, bf16[256,256]{1,0:T(8,128)(2,1)S(1)} %copy-done.7, ...), custom_call_target="tpu_custom_call" | custom-call | flops 1342177280 | bytes 4194304 | tf_op jit(solution)/shard_map/pallas_call | solution.py:98
  17.9 1.2 collective-permute-start
  19.1 5.3 %collective-permute-done.1.border = bf16[2048,128]{1,0:T(8,128)(2,1)S(1)} collective-permute-done((bf16[2048,128]{1,0:T(8,128)(2,1)S(1)}, bf16[2048,128]{1,0:T(8,128)(2,1)S(1)}, u32[]{:S(2)}, u32[]{:S(2)}) %collective-permute-start.1) | collective-permute-done | bytes 524320 | tf_op jit(solution)/shard_map/ppermute | solution.py:414
  24.4 5.4 %shard_map.200.early = bf16[2048,128]{1,0:T(8,128)(2,1)} custom-call(bf16[2048,128]{1,0:T(8,128)(2,1)S(1)} %collective-permute-done.1.border, bf16[2048,256]{1,0:T(8,128)(2,1)S(1)} %copy-done.2, bf16[2048,256]{1,0:T(8,128)(2,1)S(1)} %copy-done.3, bf16[2048,256]{1,0:T(8,128)(2,1)S(1)} %copy-done.4, f32[2048,128]{1,0:T(8,128)S(1)} %copy-done.5, ...), custom_call_target="tpu_custom_call" | custom-call | flops 1342177280 | bytes 4194304 | tf_op jit(solution)/shard_map/pallas_call | solution.py:98
  29.9 1.2 collective-permute-start.2
  31.1 5.8 %copy-done = bf16[2048,4096]{1,0:T(8,128)(2,1)S(1)} copy-done((bf16[2048,4096]{1,0:T(8,128)(2,1)S(1)}, bf16[2048,4096]{1,0:T(8,128)(2,1)}, u32[]{:S(2)}) %copy-start) | copy-done | bytes 16777240
  36.9 5.4 %shard_map.201.total = f32[2048,256]{1,0:T(8,128)S(1)} custom-call(s32[1]{0:T(128)} %bitcast.which, bf16[2048,4096]{1,0:T(8,128)(2,1)S(1)} %copy-done, bf16[2048,128]{1,0:T(8,128)(2,1)} %shard_map.199.late, bf16[2048,128]{1,0:T(8,128)(2,1)} %shard_map.200.early), custom_call_target="tpu_custom_call" | custom-call | flops 2147483648 | bytes 8388608 | tf_op jit(solution)/shard_map/pallas_call | solution.py:139
  42.3 0.1 collective-permute-done.2.early
  42.4 5.8 %copy-done.1 = bf16[2048,4096]{1,0:T(8,128)(2,1)S(1)} copy-done((bf16[2048,4096]{1,0:T(8,128)(2,1)S(1)}, bf16[2048,4096]{1,0:T(8,128)(2,1)}, u32[]{:S(2)}) %copy-start.1) | copy-done | bytes 16777240
  48.2 6.2 %shard_map.202 = bf16[2048,256]{1,0:T(8,128)(2,1)} custom-call(s32[1]{0:T(128)S(6)} %sub.3.which, bf16[2048,4096]{1,0:T(8,128)(2,1)S(1)} %copy-done.1, bf16[2048,128]{1,0:T(8,128)(2,1)} %collective-permute-done.late, bf16[2048,128]{1,0:T(8,128)(2,1)S(1)} %collective-permute-done.2.early, f32[2048,256]{1,0:T(8,128)S(1)} %shard_map.201.total, ...), custom_call_target="tpu_custom_call" | custom-call | flops 2147483648 | bytes 8388608 | tf_op jit(solution)/shard_map/pallas_call | solution.py:139
  54.4 18.7 %all-to-all-start = ((bf16[16,128,256]{2,1,0:T(8,128)(2,1)}), bf16[16,128,256]{2,1,0:T(8,128)(2,1)S(1)}, u32[]{:S(2)}, u32[]{:S(2)}) async-start(bf16[16,128,256]{2,1,0:T(8,128)(2,1)} %bitcast.1), calls=%async_computation | async-start | bytes 2097152 | tf_op jit(solution)/shard_map/all_to_all | solution.py:398
  73.1 0.0 copy-start.13
  73.2 8.3 %shard_map.203.response = f32[17,128,512]{2,1,0:T(8,128)} custom-call(bf16[16,128,256]{2,1,0:T(8,128)(2,1)} %all-to-all-done.1.source, f32[17,256]{1,0:T(8,128)S(1)} %copy-done.16, f32[17,256]{1,0:T(8,128)S(1)} %copy-done.15, bf16[512,512]{1,0:T(8,128)(2,1)S(1)} %copy-done.12, bf16[512,512]{1,0:T(8,128)(2,1)S(1)} %copy-done.11), custom_call_target="tpu_custom_call" | custom-call | flops 6845104128 | bytes 4456448 | tf_op jit(solution)/shard_map/pallas_call | solution.py:382
  81.5 14.7 %all-to-all-done.source = bf16[16,128,256]{2,1,0:T(8,128)(2,1)S(1)} async-done(((bf16[16,128,256]{2,1,0:T(8,128)(2,1)}), bf16[16,128,256]{2,1,0:T(8,128)(2,1)S(1)}, u32[]{:S(2)}, u32[]{:S(2)}) %all-to-all-start) | async-done | bytes 1048608 | tf_op jit(solution)/shard_map/all_to_all | solution.py:398
  96.2 14.9 %shard_map.204 = bf16[16,128,256]{2,1,0:T(8,128)(2,1)S(1)} custom-call(bf16[16,128,256]{2,1,0:T(8,128)(2,1)S(1)} %all-to-all-done.source, f32[17,128,512]{2,1,0:T(8,128)} %shard_map.203.response, f32[17,256]{1,0:T(8,128)S(1)} %copy-done.16, f32[17,256]{1,0:T(8,128)S(1)} %copy-done.15, f32[17,256]{1,0:T(8,128)S(1)} %copy-done.18, f32[17,256]{1,0:T(8,128)S(1)} %copy-done.17, ...), custom_call_target="tpu_custom_call" | custom-call | flops 6845104128 | bytes 4456448 | tf_op jit(solution)/shard_map/pallas_call | solution.py:382
  111.2 31.8 %all_to_all.15 = bf16[16,128,256]{2,1,0:T(8,128)(2,1)S(1)} all-to-all(bf16[16,128,256]{2,1,0:T(8,128)(2,1)S(1)} %shard_map.204), channel_id=1, replica_groups=mesh['ctx'=16,'ch'=2] {'ctx'}, dimensions={0} | all-to-all | bytes 2097152 | tf_op jit(solution)/shard_map/all_to_all | solution.py:398
  143.0 2.8 %fusion.1 = bf16[2048,256]{1,0:T(8,128)(2,1)} fusion(bf16[2048,256]{1,0:T(8,128)(2,1)} %shard_map.202, bf16[2048,256]{1,0:T(8,128)(2,1)S(1)} %copy-done.19, bf16[16,128,256]{2,1,0:T(8,128)(2,1)S(1)} %all_to_all.15, f32[2048]{0:T(1024)S(1)} %copy-done.20), kind=kLoop, calls=%fused_computation.2 | loop fusion | flops 3670016 | bytes 4202496 | tf_op jit(solution)/shard_map/convert_element_type | solution.py:432
  (37 shorter events, 0.1 us)
Async XLA Ops:
  0.0 7.7 %copy-start.3 = (bf16[2048,256]{1,0:T(8,128)(2,1)S(1)}, bf16[2048,256]{1,0:T(8,128)(2,1)}, u32[]{:S(2)}) copy-start(bf16[2048,256]{1,0:T(8,128)(2,1)} %value.3) | copy-start | bytes 3145732
  0.0 7.7 %copy-start.2 = (bf16[2048,256]{1,0:T(8,128)(2,1)S(1)}, bf16[2048,256]{1,0:T(8,128)(2,1)}, u32[]{:S(2)}) copy-start(bf16[2048,256]{1,0:T(8,128)(2,1)} %key.4) | copy-start | bytes 3145732
  0.0 11.4 %copy-start.7 = (bf16[256,256]{1,0:T(8,128)(2,1)S(1)}, bf16[256,256]{1,0:T(8,128)(2,1)}, u32[]{:S(2)}) copy-start(bf16[256,256]{1,0:T(8,128)(2,1)} %constant.31.clone.fwd_lo) | copy-start | bytes 393220
  0.0 11.4 %copy-start.8 = (bf16[256,256]{1,0:T(8,128)(2,1)S(1)}, bf16[256,256]{1,0:T(8,128)(2,1)}, u32[]{:S(2)}) copy-start(bf16[256,256]{1,0:T(8,128)(2,1)} %constant.30.clone.fwd_hi) | copy-start | bytes 393220
  0.0 11.4 %copy-start.9 = (bf16[256,128]{1,0:T(8,128)(2,1)S(1)}, bf16[256,128]{1,0:T(8,128)(2,1)}, u32[]{:S(2)}) copy-start(bf16[256,128]{1,0:T(8,128)(2,1)} %constant.33.clone.inv_lo) | copy-start | bytes 196612
  0.0 11.4 %copy-start.10 = (bf16[256,128]{1,0:T(8,128)(2,1)S(1)}, bf16[256,128]{1,0:T(8,128)(2,1)}, u32[]{:S(2)}) copy-start(bf16[256,128]{1,0:T(8,128)(2,1)} %constant.32.clone.inv_hi) | copy-start | bytes 196612
  0.0 11.4 %copy-start.4 = (bf16[2048,256]{1,0:T(8,128)(2,1)S(1)}, bf16[2048,256]{1,0:T(8,128)(2,1)}, u32[]{:S(2)}) copy-start(bf16[2048,256]{1,0:T(8,128)(2,1)} %query.3) | copy-start | bytes 3145732
  0.1 54.3 %all-to-all-start.1 = ((bf16[16,128,256]{2,1,0:T(8,128)(2,1)}), bf16[16,128,256]{2,1,0:T(8,128)(2,1)}, u32[]{:S(2)}, u32[]{:S(2)}) async-start(bf16[16,128,256]{2,1,0:T(8,128)(2,1)} %bitcast.6), calls=%async_computation.1 | async-start | bytes 2097152 | tf_op jit(solution)/shard_map/all_to_all | solution.py:398
  7.8 16.6 %collective-permute-start.1 = (bf16[2048,128]{1,0:T(8,128)(2,1)S(1)}, bf16[2048,128]{1,0:T(8,128)(2,1)S(1)}, u32[]{:S(2)}, u32[]{:S(2)}) collective-permute-start(bf16[2048,128]{1,0:T(8,128)(2,1)S(1)} %multiply_convert_fusion), channel_id=1, source_target_pairs={{0,2},{2,4},{4,6},{6,8},{8,10},{10,12},{12,14},{14,16},{16,18},{18... | collective-permute-start | bytes 1572872 | tf_op jit(solution)/shard_map/ppermute | solution.py:414
  17.9 24.4 %collective-permute-start = (bf16[2048,128]{1,0:T(8,128)(2,1)}, bf16[2048,128]{1,0:T(8,128)(2,1)}, u32[]{:S(2)}, u32[]{:S(2)}) collective-permute-start(bf16[2048,128]{1,0:T(8,128)(2,1)} %shard_map.199.late), channel_id=1, source_target_pairs={{0,1},{1,0},{2,3},{3,2},{4,5},{5,4},{6,7},{7,6},{8,9},{9,8},{10,11... | collective-permute-start | bytes 1572872 | tf_op jit(solution)/shard_map/ppermute | solution.py:418
  29.9 12.5 %collective-permute-start.2 = (bf16[2048,128]{1,0:T(8,128)(2,1)}, bf16[2048,128]{1,0:T(8,128)(2,1)S(1)}, u32[]{:S(2)}, u32[]{:S(2)}) collective-permute-start(bf16[2048,128]{1,0:T(8,128)(2,1)} %shard_map.200.early), channel_id=1, source_target_pairs={{0,1},{1,0},{2,3},{3,2},{4,5},{5,4},{6,7},{7,6},{8,9},{9,8},{10,11... | collective-permute-start | bytes 1572872 | tf_op jit(solution)/shard_map/ppermute | solution.py:420
  31.1 5.8 %copy-start = (bf16[2048,4096]{1,0:T(8,128)(2,1)S(1)}, bf16[2048,4096]{1,0:T(8,128)(2,1)}, u32[]{:S(2)}) copy-start(bf16[2048,4096]{1,0:T(8,128)(2,1)} %weight.3) | copy-start | bytes 50331652
  42.4 5.8 %copy-start.1 = (bf16[2048,4096]{1,0:T(8,128)(2,1)S(1)}, bf16[2048,4096]{1,0:T(8,128)(2,1)}, u32[]{:S(2)}) copy-start(bf16[2048,4096]{1,0:T(8,128)(2,1)} %weight.3) | copy-start | bytes 50331652
  54.3 18.7 %copy-start.11 = (bf16[512,512]{1,0:T(8,128)(2,1)S(1)}, bf16[512,512]{1,0:T(8,128)(2,1)}, u32[]{:S(2)}) copy-start(bf16[512,512]{1,0:T(8,128)(2,1)} %constant.37.clone.table_lo.fwd_lo) | copy-start | bytes 1572868
  54.3 18.7 %copy-start.12 = (bf16[512,512]{1,0:T(8,128)(2,1)S(1)}, bf16[512,512]{1,0:T(8,128)(2,1)}, u32[]{:S(2)}) copy-start(bf16[512,512]{1,0:T(8,128)(2,1)} %constant.36.clone.table_hi.fwd_hi) | copy-start | bytes 1572868
  54.3 18.7 %copy-start.15 = (f32[17,256]{1,0:T(8,128)S(1)}, f32[17,256]{1,0:T(8,128)}, u32[]{:S(2)}) copy-start(f32[17,256]{1,0:T(8,128)} %constant.35.clone.turn_im) | copy-start | bytes 52228
  54.3 18.7 %copy-start.16 = (f32[17,256]{1,0:T(8,128)S(1)}, f32[17,256]{1,0:T(8,128)}, u32[]{:S(2)}) copy-start(f32[17,256]{1,0:T(8,128)} %constant.34.clone.turn_re) | copy-start | bytes 52228
  54.4 41.8 %all-to-all-start = ((bf16[16,128,256]{2,1,0:T(8,128)(2,1)}), bf16[16,128,256]{2,1,0:T(8,128)(2,1)S(1)}, u32[]{:S(2)}, u32[]{:S(2)}) async-start(bf16[16,128,256]{2,1,0:T(8,128)(2,1)} %bitcast.1), calls=%async_computation | async-start | bytes 2097152 | tf_op jit(solution)/shard_map/all_to_all | solution.py:398
  73.1 23.1 %copy-start.13 = (bf16[512,512]{1,0:T(8,128)(2,1)S(1)}, bf16[512,512]{1,0:T(8,128)(2,1)}, u32[]{:S(2)}) copy-start(bf16[512,512]{1,0:T(8,128)(2,1)} %constant.41.clone.inv_lo) | copy-start | bytes 1572868
  73.1 23.1 %copy-start.14 = (bf16[512,512]{1,0:T(8,128)(2,1)S(1)}, bf16[512,512]{1,0:T(8,128)(2,1)}, u32[]{:S(2)}) copy-start(bf16[512,512]{1,0:T(8,128)(2,1)} %constant.40.clone.inv_hi) | copy-start | bytes 1572868
  73.1 23.1 %copy-start.17 = (f32[17,256]{1,0:T(8,128)S(1)}, f32[17,256]{1,0:T(8,128)}, u32[]{:S(2)}) copy-start(f32[17,256]{1,0:T(8,128)} %constant.39.clone.back_im) | copy-start | bytes 52228
  73.1 23.1 %copy-start.18 = (f32[17,256]{1,0:T(8,128)S(1)}, f32[17,256]{1,0:T(8,128)}, u32[]{:S(2)}) copy-start(f32[17,256]{1,0:T(8,128)} %constant.38.clone.back_re) | copy-start | bytes 52228
  111.1 31.8 %copy-start.19 = (bf16[2048,256]{1,0:T(8,128)(2,1)S(1)}, bf16[2048,256]{1,0:T(8,128)(2,1)}, u32[]{:S(2)}) copy-start(bf16[2048,256]{1,0:T(8,128)(2,1)} %param.26) | copy-start | bytes 3145732
  111.1 31.8 %copy-start.20 = (f32[2048]{0:T(1024)S(1)}, f32[2048]{0:T(1024)}, u32[]{:S(2)}) copy-start(f32[2048]{0:T(1024)} %param.29) | copy-start | bytes 24580
  (2 other events, 6.7 us)
where the time goes:
time: 146 us
  Pallas kernels  45.5 us (31%)
  starting transfers between devices  32.3 us (22%)
  blocking collectives  31.8 us (22%)
  waiting for transfers between devices  20.1 us (14%)
  local copies, waits for them, and re-layouts  12.9 us (9%)
  other arithmetic  2.91 us (2%)
    all_to_all x1, blocking collectives, exchange(): lax.all_to_all(value.reshape(groups, rows // groups, tokens), 'ctx', spli...  31.8 us
    all_to_all x2, starting transfers between devices, exchange(): lax.all_to_all(value.reshape(groups, rows // groups, tokens), 'ctx', spli...  26.3 us
    pallas_call x2, Pallas kernels, long_call(): pl.pallas_call(body, grid=(rows // block,), in_specs=specs + [whole_spec(...  23.2 us
    all_to_all x2, waiting for transfers between devices, exchange(): lax.all_to_all(value.reshape(groups, rows // groups, tokens), 'ctx', spli...  14.7 us
    unnamed x42, local copies, waits for them, and re-layouts  12.9 us
    pallas_call x2, Pallas kernels, project(): pl.pallas_call(body, grid_spec=pltpu.PrefetchScalarGridSpec(num_scalar_pr...  11.6 us
    pallas_call x2, Pallas kernels, short_conv(): pl.pallas_call(body, grid=(rows // block,), in_specs=specs + table_specs,...  10.7 us
    ppermute x1, waiting for transfers between devices, on_device(): lax.ppermute(border, 'ctx', [(i, i + 1) for i in range(groups - 1)])  5.31 us
  transfers between devices with their start and end apart: 5, of which 3 were waited for; matrix products, arithmetic and copies ran while one was open for 0% of the time, Pallas kernels for 21%

commit v1 on v0

--- a/solution.py
+++ b/solution.py
@@ -39,14 +39,15 @@
     inverse = forward.T * (2.0 / size)
     inverse[0] /= 2.0
     inverse[half] /= 2.0
-    return split_table(forward) + split_table(inverse[:, half:])
-
-
-def short_filter(window, taps, query, fwd_hi, fwd_lo, inv_hi, inv_lo):
+    return (*split_table(forward), np.concatenate(split_table(inverse[:, half:]), axis=1))
+
+
+def short_filter(window, taps, query, fwd_hi, fwd_lo, inverse):
     half = taps.shape[1]
     spec = dot(window, fwd_hi) + dot(window, fwd_lo)
     taps_hi, taps_lo = split_value(taps)
-    resp = dot(taps_hi, fwd_hi[:half]) + dot(taps_lo, fwd_hi[:half]) + dot(taps_hi, fwd_lo[:half])
+    doubled = jnp.concatenate([fwd_hi[:half], fwd_hi[:half]], axis=0)
+    resp = dot(jnp.concatenate([taps_hi, taps_lo], axis=1), doubled) + dot(taps_hi, fwd_lo[:half])
     first = lax.broadcasted_iota(jnp.int32, (taps.shape[0], half), 1) == 0
     resp_re, resp_im = resp[:, :half], resp[:, half:]
     cross = jnp.where(first, 0.0, resp_im)
@@ -56,7 +57,8 @@
         [spec_re * resp_re - spec_im * cross, spec_re * cross + spec_im * own], axis=1
     )
     prod_hi, prod_lo = split_value(prod)
-    mixed = dot(prod_hi, inv_hi) + dot(prod_lo, inv_hi) + dot(prod_hi, inv_lo)
+    both = dot(prod_hi, inverse)
+    mixed = both[:, :half] + both[:, half:] + dot(prod_lo, inverse[:, :half])
     return (query.astype(F32) * mixed).astype(BF16)
 
 
@@ -64,17 +66,18 @@
     return (key.astype(F32) * value.astype(F32)).astype(BF16)
 
 
-def late_kernel(key, value, query, taps, fwd_hi, fwd_lo, inv_hi, inv_lo, out):
+def late_kernel(key, value, query, taps, fwd_hi, fwd_lo, inverse, out, border):
     window = gate_input(key[...], value[...])
+    border[...] = window[:, query.shape[1] :]
     out[...] = short_filter(
-        window, taps[...], query[...], fwd_hi[...], fwd_lo[...], inv_hi[...], inv_lo[...]
-    )
-
-
-def early_kernel(border, key, value, query, taps, fwd_hi, fwd_lo, inv_hi, inv_lo, out):
+        window, taps[...], query[...], fwd_hi[...], fwd_lo[...], inverse[...]
+    )
+
+
+def early_kernel(border, key, value, query, taps, fwd_hi, fwd_lo, inverse, out):
     window = jnp.concatenate([border[...], gate_input(key[...], value[...])], axis=1)
     out[...] = short_filter(
-        window, taps[...], query[...], fwd_hi[...], fwd_lo[...], inv_hi[...], inv_lo[...]
+        window, taps[...], query[...], fwd_hi[...], fwd_lo[...], inverse[...]
     )
 
 
@@ -82,71 +85,141 @@
     return pl.BlockSpec(array.shape, lambda *_: (0,) * array.ndim)
 
 
-def short_conv(border, key, value, query, taps, tables):
+def short_conv(border, key, value, query, taps, tables, block=1024):
     rows, tokens = key.shape
     half = tokens // 2
-    block = min(rows, 512)
+    block = min(rows, block)
     table_specs = [whole_spec(t) for t in tables]
     full = pl.BlockSpec((block, tokens), lambda i: (i, 0))
     left = pl.BlockSpec((block, half), lambda i: (i, 0))
     right = pl.BlockSpec((block, half), lambda i: (i, 1))
     if border is None:
-        body, specs, args = late_kernel, [full, full, right, left], (key, value, query, taps)
+        body, specs, outs = late_kernel, [full, full, right, left], 2
+        args = (key, value, query, taps)
     else:
-        body, specs = early_kernel, [left, left, left, left, left]
+        body, specs, outs = early_kernel, [left, left, left, left, left], 1
         args = (border, key, value, query, taps)
     return pl.pallas_call(
         body,
         grid=(rows // block,),
         in_specs=specs + table_specs,
-        out_specs=left,
-        out_shape=jax.ShapeDtypeStruct((rows, half), BF16),
-        compiler_params=pltpu.CompilerParams(vmem_limit_bytes=32 * MIB),
+        out_specs=[left] * outs,
+        out_shape=[jax.ShapeDtypeStruct((rows, half), BF16)] * outs,
+        compiler_params=pltpu.CompilerParams(vmem_limit_bytes=60 * MIB),
         cost_estimate=pl.CostEstimate(
-            flops=10 * rows * tokens * tokens, bytes_accessed=8 * rows * tokens, transcendentals=0
+            flops=50 * rows * tokens * tokens, bytes_accessed=8 * rows * tokens, transcendentals=0
         ),
     )(*args, *tables)
 
 
-def own_kernel(which, weight, late, early, out):
+def own_kernel(which, weight, late, early, late_out, early_out):
     del which
-    out[...] = dot(weight[...], jnp.concatenate([early[...], late[...]], axis=1))
-
-
-def other_kernel(which, weight, late, early, total, key, out):
-    del which
-    values = total[...] + dot(weight[...], jnp.concatenate([early[...], late[...]], axis=1))
-    out[...] = (key[...].astype(F32) * values).astype(BF16)
-
-
-def project(which, weight, late, early, total=None, key=None):
-    rows, depth = weight.shape[0], late.shape[0]
     half = late.shape[1]
-    block = min(rows, 256)
-    moving = pl.BlockSpec((block, 2 * half), lambda i, w: (i, 0))
-    specs = [
-        pl.BlockSpec((block, depth), lambda i, w: (i, w[0])),
-        pl.BlockSpec((depth, half), lambda i, w: (0, 0)),
-        pl.BlockSpec((depth, half), lambda i, w: (0, 0)),
-    ]
-    args = [weight, late, early]
-    if total is None:
-        body, dtype = own_kernel, F32
-    else:
-        body, dtype = other_kernel, BF16
-        specs += [moving, moving]
-        args += [total, key]
+    found = dot(weight[...], jnp.concatenate([late[...], early[...]], axis=1))
+
+    @pl.when(pl.program_id(0) == 0)
+    def _():
+        late_out[...] = found[:, :half]
+        early_out[...] = found[:, half:]
+
+    @pl.when(pl.program_id(0) > 0)
+    def _():
+        late_out[...] += found[:, :half]
+        early_out[...] += found[:, half:]
+
+
+def other_kernel(pairs, which, weight, late, early, late_total, early_total, key, out, *refs):
+    *pieces, sums = refs
+    half = late.shape[1]
+    found = dot(weight[...], jnp.concatenate([early[...], late[...]], axis=1))
+
+    @pl.when(pl.program_id(0) == 0)
+    def _():
+        sums[:, :half] = early_total[...] + found[:, :half]
+        sums[:, half:] = late_total[...] + found[:, half:]
+
+    @pl.when(pl.program_id(0) > 0)
+    def _():
+        sums[...] += found
+
+    @pl.when(pl.program_id(0) == pl.num_programs(0) - 1)
+    def _():
+        out[...] = (key[...].astype(F32) * sums[...]).astype(BF16)
+        chip, core = which[1], which[2]
+        for i, piece in enumerate(pieces):
+            chunk, rel = divmod(i, pairs)
+            rows = piece.shape[1]
+            for slot in range(2):
+                piece[slot] = out[chunk_rows(chip ^ rel, core ^ slot, chunk, rows), :]
+
+
+def chunk_rows(chip, core, chunk, rows):
+    start = ((chip * 2 + core) * CHUNKS + chunk) * rows
+    return pl.ds(pl.multiple_of(start, rows), rows)
+
+
+CHUNKS = 2
+DEPTH = 1024
+
+
+def project_own(which, weight, late, early):
+    rows, (depth, half) = weight.shape[0], late.shape
+    block = min(depth, DEPTH)
+    steps = depth // block
+    moving = pl.BlockSpec((block, half), lambda i, w: (i, 0))
+    fixed = pl.BlockSpec((rows, half), lambda i, w: (0, 0))
     return pl.pallas_call(
-        body,
+        own_kernel,
         grid_spec=pltpu.PrefetchScalarGridSpec(
-            num_scalar_prefetch=1, grid=(rows // block,), in_specs=specs, out_specs=moving
-        ),
-        out_shape=jax.ShapeDtypeStruct((rows, 2 * half), dtype),
-        compiler_params=pltpu.CompilerParams(vmem_limit_bytes=32 * MIB),
+            num_scalar_prefetch=1,
+            grid=(steps,),
+            in_specs=[
+                pl.BlockSpec((rows, block), lambda i, w: (0, w[0] * steps + i)),
+                moving,
+                moving,
+            ],
+            out_specs=[fixed, fixed],
+        ),
+        out_shape=[jax.ShapeDtypeStruct((rows, half), F32)] * 2,
+        compiler_params=pltpu.CompilerParams(vmem_limit_bytes=56 * MIB),
         cost_estimate=pl.CostEstimate(
             flops=4 * rows * depth * half, bytes_accessed=2 * rows * depth, transcendentals=0
         ),
-    )(which, *args)
+    )(which, weight, late, early)
+
+
+def project_other(where, weight, late, early, late_total, early_total, key, pairs):
+    rows, (depth, half) = weight.shape[0], late.shape
+    block = min(depth, DEPTH)
+    steps = depth // block
+    moving = pl.BlockSpec((block, half), lambda i, w: (i, 0))
+    fixed = pl.BlockSpec((rows, half), lambda i, w: (0, 0))
+    full = pl.BlockSpec((rows, 2 * half), lambda i, w: (0, 0))
+    shape = (2, rows // (2 * max(pairs, 1) * CHUNKS), 2 * half)
+    piece = pl.BlockSpec(shape, lambda i, w: (0, 0, 0))
+    return pl.pallas_call(
+        functools.partial(other_kernel, pairs),
+        grid_spec=pltpu.PrefetchScalarGridSpec(
+            num_scalar_prefetch=1,
+            grid=(steps,),
+            in_specs=[
+                pl.BlockSpec((rows, block), lambda i, w: (0, w[0] * steps + i)),
+                moving,
+                moving,
+                fixed,
+                fixed,
+                full,
+            ],
+            out_specs=[full] + [piece] * (pairs * CHUNKS),
+            scratch_shapes=[pltpu.VMEM((rows, 2 * half), F32)],
+        ),
+        out_shape=[jax.ShapeDtypeStruct((rows, 2 * half), BF16)]
+        + [jax.ShapeDtypeStruct(shape, BF16)] * (pairs * CHUNKS),
+        compiler_params=pltpu.CompilerParams(vmem_limit_bytes=60 * MIB),
+        cost_estimate=pl.CostEstimate(
+            flops=24 * rows * depth * half, bytes_accessed=2 * rows * depth, transcendentals=0
+        ),
+    )(where, weight, late, early, late_total, early_total, key)
 
 
 def turn(value, num, den):
@@ -278,7 +351,7 @@
 SUBS = 16
 
 
-def forward_slabs(source, turn_re, turn_im, high, low):
+def forward_slabs(source, turn_re, turn_im, parts):
     slabs, rows, tokens = source.shape
     lanes = min(tokens, LANES)
     subs = min(rows, SUBS)
@@ -296,50 +369,55 @@
                     out = (re * cos - im * sin, re * sin + im * cos)
                 for part, value in enumerate(out):
                     where = slice(part * tokens + lane, part * tokens + lane + lanes)
-                    hi, lo = split_value(value)
-                    high[k, at, where] = hi
-                    low[k, at, where] = lo
+                    store_split(parts, (k, at, where), value)
             return carry
 
         lax.fori_loop(0, rows // subs, tile, 0)
 
 
-def product3(high, low, table_hi, table_lo):
-    a, b = high[...], low[...]
-    shape = a.shape
-    a = a.reshape(shape[0] * shape[1], shape[2])
-    b = b.reshape(shape[0] * shape[1], shape[2])
-    out = dot(a, table_hi[...]) + dot(b, table_hi[...]) + dot(a, table_lo[...])
-    return out.reshape(shape[0], shape[1], -1)
-
-
-def response_kernel(source, turn_re, turn_im, table_hi, table_lo, out, high, low):
-    forward_slabs(source, turn_re, turn_im, high, low)
-    out[...] = product3(high, low, table_hi, table_lo)
-
-
-def convolve_kernel(
-    source, response, turn_re, turn_im, back_re, back_im, fwd_hi, fwd_lo, inv_hi, inv_lo, out, high, low, spec
-):
-    slabs, rows, tokens = source.shape
-    lanes = min(tokens, LANES)
-    subs = min(rows, SUBS)
-    forward_slabs(source, turn_re, turn_im, high, low)
-    spec[...] = product3(high, low, fwd_hi, fwd_lo)
-
-    def multiply(k, carry):
+def store_split(parts, where, value):
+    high = value.astype(BF16)
+    parts[0][where] = high
+    if len(parts) > 1:
+        parts[1][where] = (value - high.astype(F32)).astype(BF16)
+
+
+def product(parts, tables):
+    slabs, rows, depth = parts[0].shape
+    flat = [p[...].reshape(slabs * rows, depth) for p in parts]
+    out = dot(flat[0], tables[0][...])
+    for left, right in zip(flat[1:], tables):
+        out += dot(left, right[...])
+    for right in tables[1:]:
+        out += dot(flat[0], right[...])
+    return out.reshape(slabs, rows, depth)
+
+
+def response_kernel(source, turn_re, turn_im, high, low, out, *parts):
+    forward_slabs(source, turn_re, turn_im, parts)
+    out[...] = product(parts, (high, low))
+
+
+def multiply(spec, response, parts):
+    tokens = spec.shape[2] // 2
+
+    def one(k, carry):
         sig_re, sig_im = spec[k, :, :tokens], spec[k, :, tokens:]
         res_re, res_im = response[k, :, :tokens], response[k, :, tokens:]
         for part, value in enumerate(
             (sig_re * res_re - sig_im * res_im, sig_re * res_im + sig_im * res_re)
         ):
-            hi, lo = split_value(value)
-            high[k, :, part * tokens : (part + 1) * tokens] = hi
-            low[k, :, part * tokens : (part + 1) * tokens] = lo
+            where = (k, slice(None), slice(part * tokens, (part + 1) * tokens))
+            store_split(parts, where, value)
         return carry
 
-    lax.fori_loop(0, slabs + 1, multiply, 0)
-    spec[...] = product3(high, low, inv_hi, inv_lo)
+    lax.fori_loop(0, spec.shape[0], one, 0)
+
+
+def back_slabs(spec, back_re, back_im, out):
+    slabs, rows, tokens = out.shape
+    lanes = min(tokens, LANES)
+    subs = min(rows, SUBS)
     for lane in range(0, tokens, lanes):
 
         def tile(step, carry, lane=lane):
@@ -361,36 +439,143 @@
         lax.fori_loop(0, rows // subs, tile, 0)
 
 
-def long_call(source, response, tables, start=0, count=None):
-    slabs, rows, tokens = source.shape
-    block = min(rows, 32)
+def convolve_kernel(
+    block, source, response, turn_re, turn_im, back_re, back_im, forward, inverse, out, spec, part, held, sem
+):
+    convolve(block, source, response, (turn_re, turn_im, back_re, back_im), forward, inverse, out, spec, part, held, sem)
+
+
+def convolve(block, source, response, turns, forward, inverse, out, spec, part, held, sem):
+    rows = source.shape[1]
+    turn_re, turn_im, back_re, back_im = turns
+    copies = [
+        pltpu.make_async_copy(
+            response.at[:, pl.ds(i * block, block), :], held.at[i], sem.at[i]
+        )
+        for i in range(rows // block)
+    ]
+    for copy in copies:
+        copy.start()
+    for i, copy in enumerate(copies):
+        at = pl.ds(i * block, block)
+        forward_slabs(source.at[:, at, :], turn_re, turn_im, [part])
+        spec[...] = product([part], (forward,))
+        copy.wait()
+        multiply(spec, held.at[i], [part])
+        spec[...] = product([part], (inverse,))
+        back_slabs(spec, back_re, back_im, out.at[:, at, :])
+
+
+def pieces_kernel(pairs, block, chunk, where, *refs):
+    own, (other, response, *turns, forward, inverse) = refs[:pairs], refs[pairs : pairs + 8]
+    outs, (source, out, *scratch) = refs[pairs + 8 : 2 * pairs + 8], refs[2 * pairs + 8 :]
+    chip, core = where[1], where[2]
+    for rel in range(pairs):
+        source[2 * (chip ^ rel) + core] = own[rel][0]
+        source[2 * (chip ^ rel) + 1 - core] = other[rel]
+    rows = source.shape[1]
+    response = response.at[:, pl.ds(chunk * rows, rows), :]
+    convolve(block, source, response, turns, forward, inverse, out, *scratch)
+    for rel in range(pairs):
+        for slot in range(2):
+            outs[rel][slot] = out[2 * (chip ^ rel) + (core ^ slot)]
+
+
+def convolve_call(where, source, response, tables, chunk=None, block=64):
+    if chunk is None:
+        slabs, rows, tokens = source.shape
+    else:
+        slabs, (_, rows, tokens) = 2 * len(source[0]), source[1].shape
+    block = min(rows, block)
     turns, forward, inverse = tables
-    if response is None:
-        body, given = response_kernel, [*turns[:2], *forward]
+    here = pl.BlockSpec(memory_space=pltpu.VMEM)
+    given = [*turns, forward[0], inverse[0]]
+    specs = [pl.BlockSpec(memory_space=pl.ANY)] + [here] * len(given)
+    wide = (slabs + 1, block, 2 * tokens)
+    scratch = [
+        pltpu.VMEM(wide, F32),
+        pltpu.VMEM(wide, BF16),
+        pltpu.VMEM((rows // block, *wide), F32),
+        pltpu.SemaphoreType.DMA((rows // block,)),
+    ]
+    if chunk is None:
+        body = functools.partial(convolve_kernel, block)
+        args, specs = [source, response, *given], [here] + specs
+        out_specs, out_shape = here, jax.ShapeDtypeStruct((slabs, rows, tokens), BF16)
     else:
-        body, given = convolve_kernel, [*turns, *forward, *inverse]
-    data = pl.BlockSpec((slabs, block, tokens), lambda i: (0, i, 0))
-    wide = pl.BlockSpec((slabs + 1, block, 2 * tokens), lambda i: (0, i, 0))
-    scratch = [pltpu.VMEM((slabs + 1, block, 2 * tokens), t) for t in (BF16, BF16, F32)]
-    flops = 12 * (slabs + 1) * rows * 4 * tokens * tokens
-    if response is None:
-        out_spec, out_shape, scratch = wide, ((slabs + 1, rows, 2 * tokens), F32), scratch[:2]
-        args, specs = [source], [data]
-    else:
-        out_spec, out_shape = data, ((slabs, rows, tokens), BF16)
-        args, specs = [source, response], [data, wide]
+        pairs = len(source[0])
+        body = functools.partial(pieces_kernel, pairs, block, chunk)
+        args = [where, *source[0], source[1], response, *given]
+        specs = [pl.BlockSpec(memory_space=pltpu.SMEM)] + [here] * (pairs + 1) + specs
+        out_specs = [here] * pairs
+        out_shape = [jax.ShapeDtypeStruct((2, rows, tokens), BF16)] * pairs
+        scratch = [pltpu.VMEM((slabs, rows, tokens), BF16)] * 2 + scratch
     return pl.pallas_call(
         body,
-        grid=(rows // block,),
-        in_specs=specs + [whole_spec(t) for t in given],
-        out_specs=out_spec,
-        out_shape=jax.ShapeDtypeStruct(*out_shape),
+        in_specs=specs,
+        out_specs=out_specs,
+        out_shape=out_shape,
         scratch_shapes=scratch,
         compiler_params=pltpu.CompilerParams(vmem_limit_bytes=48 * MIB),
         cost_estimate=pl.CostEstimate(
-            flops=flops, bytes_accessed=8 * (slabs + 1) * rows * tokens, transcendentals=0
-        ),
-    )(*args, *given)
+            flops=16 * (slabs + 1) * rows * tokens * tokens, bytes_accessed=rows, transcendentals=0
+        ),
+    )(*args)
+
+
+def response_call(source, tables, block=32):
+    slabs, rows, tokens = source.shape
+    block = min(rows, block)
+    turns, forward, _ = tables
+    given = [*turns[:2], *forward]
+    wide = (slabs + 1, block, 2 * tokens)
+    return pl.pallas_call(
+        response_kernel,
+        grid=(rows // block,),
+        in_specs=[pl.BlockSpec((slabs, block, tokens), lambda i: (0, i, 0))]
+        + [whole_spec(t) for t in given],
+        out_specs=pl.BlockSpec(wide, lambda i: (0, i, 0)),
+        out_shape=jax.ShapeDtypeStruct((slabs + 1, rows, 2 * tokens), F32),
+        scratch_shapes=[pltpu.VMEM(wide, BF16)] * 2,
+        compiler_params=pltpu.CompilerParams(vmem_limit_bytes=60 * MIB),
+        cost_estimate=pl.CostEstimate(
+            flops=24 * (slabs + 1) * rows * tokens * tokens, bytes_accessed=rows, transcendentals=0
+        ),
+    )(source, *given)
+
+
+def gate_kernel(pairs, where, query, skip, given, *refs):
+    pieces, (out, rows_out, sem) = refs[: CHUNKS * (pairs + 1)], refs[CHUNKS * (pairs + 1) :]
+    chip, core = where[1], where[2]
+    rows = pieces[0].shape[1]
+    chip_rows = 2 * CHUNKS * rows
+    copies = []
+    for rel in range(pairs):
+        for chunk in range(CHUNKS):
+            own, other = pieces[chunk * (pairs + 1) + rel], pieces[chunk * (pairs + 1) + pairs]
+            for slot, part in ((0, own[0]), (1, other[rel])):
+                at = chunk_rows(chip ^ rel, core ^ slot, chunk, rows)
+                direct = skip[at, :1] * given[at, :].astype(F32)
+                result = query[at, :].astype(F32) * (part.astype(F32) + direct)
+                rows_out[at, :] = result.astype(BF16)
+        at = pl.ds(pl.multiple_of((chip ^ rel) * chip_rows, chip_rows), chip_rows)
+        copies.append(pltpu.make_async_copy(rows_out.at[at, :], out.at[at, :], sem.at[rel]))
+        copies[-1].start()
+    for copy in copies:
+        copy.wait()
+
+
+def gate_call(where, query, skip, given, pieces, pairs):
+    here = pl.BlockSpec(memory_space=pltpu.VMEM)
+    flat = [p for own, other in pieces for p in (*own, other)]
+    return pl.pallas_call(
+        functools.partial(gate_kernel, pairs),
+        in_specs=[pl.BlockSpec(memory_space=pltpu.SMEM)] + [here] * (3 + len(flat)),
+        out_specs=pl.BlockSpec(memory_space=pl.ANY),
+        out_shape=jax.ShapeDtypeStruct(query.shape, BF16),
+        scratch_shapes=[pltpu.VMEM(query.shape, BF16), pltpu.SemaphoreType.DMA((pairs,))],
+        compiler_params=pltpu.CompilerParams(vmem_limit_bytes=16 * MIB),
+    )(where, query, skip, given, *flat)
 
 
 def exchange(value, groups):
@@ -398,6 +583,36 @@
     return lax.all_to_all(
         value.reshape(groups, rows // groups, tokens), "ctx", split_axis=0, concat_axis=0, tiled=True
     )
+
+
+MOST_PAIRS = 0
+
+
+def second_kernel(*refs):
+    *pieces, out = refs
+    for rel, piece in enumerate(pieces):
+        out[rel] = piece[1]
+
+
+def second_slots(pieces):
+    here = pl.BlockSpec(memory_space=pltpu.VMEM)
+    return pl.pallas_call(
+        second_kernel,
+        in_specs=[here] * len(pieces),
+        out_specs=here,
+        out_shape=jax.ShapeDtypeStruct((len(pieces), *pieces[0].shape[1:]), BF16),
+        cost_estimate=pl.CostEstimate(
+            flops=pieces[0].size, bytes_accessed=pieces[0].size, transcendentals=0
+        ),
+    )(*pieces)
+
+
+def to_chips(pieces, groups):
+    found = [pieces[0]]
+    for rel in range(1, len(pieces)):
+        found.append(lax.ppermute(pieces[rel], "ctx", [(i, i ^ (2 * rel)) for i in range(groups)]))
+    second = second_slots(found)
+    return found, lax.ppermute(second, "ctx", [(i, i ^ 1) for i in range(groups)])
 
 
 def on_device(
@@ -406,30 +621,43 @@
     rows, tokens = mr_key.shape
     half = tokens // 2
     groups = lax.axis_size("ctx")
+    pairs = groups // 2 if groups // 2 <= MOST_PAIRS else 0
     short = short_tables(tokens)
     tables = long_tables(groups, tokens)
     swap = [(0, 1), (1, 0)]
-
-    border = gate_input(mr_key[:, half:], mr_value[:, half:])
+    mine = lax.axis_index("ch").astype(jnp.int32)
+    slab = lax.axis_index("ctx").astype(jnp.int32)
+    own = jnp.stack([mine, slab // 2, slab % 2])
+    where = jnp.stack([1 - mine, slab // 2, slab % 2])
+
+    late, border = short_conv(None, mr_key, mr_value, mr_query, mr_filter, short)
     border = lax.ppermute(border, "ctx", [(i, i + 1) for i in range(groups - 1)])
+    other_late = lax.ppermute(late, "ch", swap)
+    li_filter, late = lax.optimization_barrier((li_filter, late))
     filter_part = exchange(li_filter, groups)
-
-    late = short_conv(None, mr_key, mr_value, mr_query, mr_filter, short)
-    other_late = lax.ppermute(late, "ch", swap)
-    early = short_conv(border, mr_key, mr_value, mr_query, mr_filter, short)
+    (early,) = short_conv(border, mr_key, mr_value, mr_query, mr_filter, short)
     other_early = lax.ppermute(early, "ch", swap)
 
-    me = lax.axis_index("ch").astype(jnp.int32).reshape(1)
-    total = project(me, proj_weight, late, early)
-    li_input = project(1 - me, proj_weight, other_late, other_early, total, li_key)
-
-    response = long_call(filter_part, None, tables)
-    long_part = long_call(exchange(li_input, groups), response, tables)
-    long_local = exchange(long_part.reshape(rows, tokens), groups).reshape(rows, tokens)
-    gated_out = li_query.astype(F32) * (
-        long_local.astype(F32) + li_skip[:, None] * li_input.astype(F32)
-    )
-    return gated_out.astype(BF16)
+    late_total, early_total = project_own(own, proj_weight, late, early)
+    li_input, *pieces = project_other(
+        where, proj_weight, other_late, other_early, late_total, early_total, li_key, pairs
+    )
+    response = response_call(filter_part, tables)
+    if not pairs:
+        long_part = convolve_call(where, exchange(li_input, groups), response, tables)
+        long_local = exchange(long_part.reshape(rows, tokens), groups).reshape(rows, tokens)
+        gated_out = li_query.astype(F32) * (
+            long_local.astype(F32) + li_skip[:, None] * li_input.astype(F32)
+        )
+        return gated_out.astype(BF16)
+
+    arrived = [to_chips(pieces[c * pairs : (c + 1) * pairs], groups) for c in range(CHUNKS)]
+    returned = []
+    for chunk, source in enumerate(arrived):
+        back = convolve_call(where, source, response, tables, chunk)
+        returned.append(to_chips(back, groups))
+    skip = jnp.broadcast_to(li_skip[:, None], (rows, 128))
+    return gate_call(where, li_query, skip, li_input, returned, pairs)
 
 
 def solution(mesh):

time: 146 us -> 114 us (0.78)
  starting transfers between devices: 32.3 us -> 18.3 us
  local copies, waits for them, and re-layouts: 12.9 us -> 1.65 us
  Pallas kernels: 45.5 us -> 39.8 us
  waiting for transfers between devices: 20.1 us -> 18.6 us
    all_to_all x2, starting transfers between devices: 26.3 us -> 11.3 us  [exchange(): lax.all_to_all(value.reshape(groups, rows // groups, tokens), 'ctx', spli...]
    unnamed x42 -> x26, local copies, waits for them, and re-layouts: 12.9 us -> 1.65 us
    ppermute x1, waiting for transfers between devices: 5.31 us -> 0.13 us  [on_device(): lax.ppermute(border, 'ctx', [(i, i + 1) for i in range(groups - 1)])]
    ppermute x1, waiting for transfers between devices: 0.08 us -> 4.15 us  [on_device(): other_early = lax.ppermute(early, 'ch', swap)]
    pallas_call x4, Pallas kernels: 34.8 us -> 31.1 us  [the longest x1 8.71 us: response_call(): pl.pallas_call(response_kernel, grid=(rows // block,), in_specs=[pl.Block...]
    pallas_call x2, Pallas kernels: 10.7 us -> 8.71 us  [short_conv(): pl.pallas_call(body, grid=(rows // block,), in_specs=specs + table_specs,...]
  transfers between devices with their start and end apart: 5 -> 5, of which waited for: 3 -> 3; matrix products, arithmetic and copies ran while one was open for 0% -> 1% of each run, Pallas kernels for 21% -> 25%
where the time goes in v1:
time: 114 us; the launch traced here: 113 us
  Pallas kernels  39.8 us (35%)
  blocking collectives  31.8 us (28%)
  waiting for transfers between devices  18.6 us (16%)
  starting transfers between devices  18.3 us (16%)
  other arithmetic  2.81 us (2%)
  local copies, waits for them, and re-layouts  1.65 us (1%)
    all_to_all x1, blocking collectives, exchange(): lax.all_to_all(value.reshape(groups, rows // groups, tokens), 'ctx', spli...  31.8 us
    all_to_all x2, waiting for transfers between devices, exchange(): lax.all_to_all(value.reshape(groups, rows // groups, tokens), 'ctx', spli...  14.3 us
    all_to_all x2, starting transfers between devices, exchange(): lax.all_to_all(value.reshape(groups, rows // groups, tokens), 'ctx', spli...  11.3 us
    pallas_call x2, Pallas kernels, short_conv(): pl.pallas_call(body, grid=(rows // block,), in_specs=specs + table_specs,...  8.71 us
    pallas_call x1, Pallas kernels, response_call(): pl.pallas_call(response_kernel, grid=(rows // block,), in_specs=[pl.Block...  8.71 us
    pallas_call x1, Pallas kernels, project_other(): pl.pallas_call(functools.partial(other_kernel, pairs), grid_spec=pltpu.Pr...  8.18 us
    pallas_call x1, Pallas kernels, project_own(): pl.pallas_call(own_kernel, grid_spec=pltpu.PrefetchScalarGridSpec(num_sca...  7.18 us
    pallas_call x1, Pallas kernels, convolve_call(): pl.pallas_call(body, in_specs=specs, out_specs=out_specs, out_shape=out_s...  7.04 us
  transfers between devices with their start and end apart: 5, of which 3 were waited for; matrix products, arithmetic and copies ran while one was open for 1% of the time, Pallas kernels for 25%

profile of v1, /device:TPU:1, one launch (start us, length us, event | category | flops | bytes accessed | tf_op | source)
XLA Modules:
  0.0 113.2 jit_solution(2855554446158586786)
XLA Ops:
  0.0 4.4 %shard_map.181 = (bf16[2048,128]{1,0:T(8,128)(2,1)}, bf16[2048,128]{1,0:T(8,128)(2,1)}) custom-call(bf16[2048,256]{1,0:T(8,128)(2,1)} %key.4, bf16[2048,256]{1,0:T(8,128)(2,1)} %value.3, bf16[2048,256]{1,0:T(8,128)(2,1)} %query.3, f32[2048,128]{1,0:T(8,128)} %taps.3, bf16[256,256]{1,0:T(8,128)(2,1)} %constant.57.clone.fwd_hi, ...), custom_call_target="tpu_custom_call" | custom-call | flops 6710886400 | bytes 4194304 | tf_op jit(solution)/shard_map/pallas_call | solution.py:102
  4.4 4.5 %collective-permute-start.1 = (bf16[2048,128]{1,0:T(8,128)(2,1)}, bf16[2048,128]{1,0:T(8,128)(2,1)S(1)}, u32[]{:S(2)}, u32[]{:S(2)}) collective-permute-start(bf16[2048,128]{1,0:T(8,128)(2,1)} %get-tuple-element.12), channel_id=1, source_target_pairs={{0,2},{2,4},{4,6},{6,8},{8,10},{10,12},{12,14},{14,16},{16,18},{18... | collective-permute-start | bytes 1572872 | tf_op jit(solution)/shard_map/ppermute | solution.py:634
  8.9 1.3 %collective-permute-start = (bf16[2048,128]{1,0:T(8,128)(2,1)}, bf16[2048,128]{1,0:T(8,128)(2,1)S(1)}, u32[]{:S(2)}, u32[]{:S(2)}) collective-permute-start(bf16[2048,128]{1,0:T(8,128)(2,1)} %get-tuple-element.13.late), channel_id=1, source_target_pairs={{0,1},{1,0},{2,3},{3,2},{4,5},{5,4},{6,7},{7,6},{8,9},{9,8},{10,11... | collective-permute-start | bytes 1572872 | tf_op jit(solution)/shard_map/ppermute | solution.py:635
  10.2 5.0 %all-to-all-start.1 = ((bf16[16,128,256]{2,1,0:T(8,128)(2,1)}), bf16[16,128,256]{2,1,0:T(8,128)(2,1)S(1)}, u32[]{:S(2)}, u32[]{:S(2)}) async-start(bf16[16,128,256]{2,1,0:T(8,128)(2,1)} %bitcast.5), calls=%async_computation.1 | async-start | bytes 2097152 | tf_op jit(solution)/shard_map/all_to_all | solution.py:583
  15.2 0.1 collective-permute-done.1.border
  15.4 0.8 copy-done.12
  16.2 4.3 %shard_map.182.early = bf16[2048,128]{1,0:T(8,128)(2,1)} custom-call(bf16[2048,128]{1,0:T(8,128)(2,1)} %copy-done.12, bf16[2048,256]{1,0:T(8,128)(2,1)} %key.4, bf16[2048,256]{1,0:T(8,128)(2,1)} %value.3, bf16[2048,256]{1,0:T(8,128)(2,1)} %query.3, f32[2048,128]{1,0:T(8,128)} %taps.3, bf16[256,256]{1,0:T(8,128)(2,1)} %constant.57.clone.fwd_hi, ...), custom_call_target="tpu_custom_call" | custom-call | flops 6710886400 | bytes 4194304 | tf_op jit(solution)/shard_map/pallas_call | solution.py:102
  20.5 1.2 %collective-permute-start.2 = (bf16[2048,128]{1,0:T(8,128)(2,1)}, bf16[2048,128]{1,0:T(8,128)(2,1)S(1)}, u32[]{:S(2)}, u32[]{:S(2)}) collective-permute-start(bf16[2048,128]{1,0:T(8,128)(2,1)} %shard_map.182.early), channel_id=1, source_target_pairs={{0,1},{1,0},{2,3},{3,2},{4,5},{5,4},{6,7},{7,6},{8,9},{9,8},{10,11... | collective-permute-start | bytes 1572872 | tf_op jit(solution)/shard_map/ppermute | solution.py:639
  21.7 0.7 add_add_fusion.which
  22.3 0.6 add_add_fusion.1.which
  22.9 7.2 %shard_map.183 = (f32[2048,128]{1,0:T(8,128)}, f32[2048,128]{1,0:T(8,128)}) custom-call(s32[3]{0:T(128)} %add_add_fusion.1.which, bf16[2048,4096]{1,0:T(8,128)(2,1)} %weight.3, bf16[2048,128]{1,0:T(8,128)(2,1)} %get-tuple-element.13.late, bf16[2048,128]{1,0:T(8,128)(2,1)} %shard_map.182.early), custom_call_target="tpu_custom_call" | custom-call | flops 2147483648 | bytes 8388608 | tf_op jit(solution)/shard_map/pallas_call | solution.py:171
  30.1 4.2 %collective-permute-done.2.early = bf16[2048,128]{1,0:T(8,128)(2,1)S(1)} collective-permute-done((bf16[2048,128]{1,0:T(8,128)(2,1)}, bf16[2048,128]{1,0:T(8,128)(2,1)S(1)}, u32[]{:S(2)}, u32[]{:S(2)}) %collective-permute-start.2) | collective-permute-done | bytes 524320 | tf_op jit(solution)/shard_map/ppermute | solution.py:639
  34.3 0.8 copy-done.11
  35.1 8.2 %shard_map.184 = bf16[2048,256]{1,0:T(8,128)(2,1)} custom-call(s32[3]{0:T(128)} %add_add_fusion.which, bf16[2048,4096]{1,0:T(8,128)(2,1)} %weight.3, bf16[2048,128]{1,0:T(8,128)(2,1)} %copy-done.10, bf16[2048,128]{1,0:T(8,128)(2,1)} %copy-done.11, f32[2048,128]{1,0:T(8,128)} %get-tuple-element.14.late_total, f32[2048,128]{1,0:T(8,128)} %get-tuple-element.15.early_total, ...), custom_call_target="tpu_custom_call" | custom-call | flops 12884901888 | bytes 8388608 | tf_op jit(solution)/shard_map/pallas_call | solution.py:200
  43.2 6.3 %all-to-all-start = ((bf16[16,128,256]{2,1,0:T(8,128)(2,1)}), bf16[16,128,256]{2,1,0:T(8,128)(2,1)S(1)}, u32[]{:S(2)}, u32[]{:S(2)}) async-start(bf16[16,128,256]{2,1,0:T(8,128)(2,1)} %bitcast.9), calls=%async_computation | async-start | bytes 2097152 | tf_op jit(solution)/shard_map/all_to_all | solution.py:583
  49.6 0.0 copy-start
  49.6 0.0 copy-start.1
  49.6 0.0 copy-start.2
  49.6 0.0 copy-start.3
  49.6 8.7 %shard_map.185.response = f32[17,128,512]{2,1,0:T(8,128)} custom-call(bf16[16,128,256]{2,1,0:T(8,128)(2,1)} %copy-done.7, f32[17,256]{1,0:T(8,128)} %constant.60.clone.turn_re, f32[17,256]{1,0:T(8,128)} %constant.61.clone.turn_im, bf16[512,512]{1,0:T(8,128)(2,1)} %constant.62.clone.high.forward, bf16[512,512]{1,0:T(8,128)(2,1)} %constant.63.clone.low), custom_call_target="tpu_custom_call" | custom-call | flops 3422552064 | bytes 128 | tf_op jit(solution)/shard_map/pallas_call | solution.py:532
  58.3 14.3 %all-to-all-done.source = bf16[16,128,256]{2,1,0:T(8,128)(2,1)S(1)} async-done(((bf16[16,128,256]{2,1,0:T(8,128)(2,1)}), bf16[16,128,256]{2,1,0:T(8,128)(2,1)S(1)}, u32[]{:S(2)}, u32[]{:S(2)}) %all-to-all-start) | async-done | bytes 1048608 | tf_op jit(solution)/shard_map/all_to_all | solution.py:583
  72.7 7.0 %shard_map.186 = bf16[16,128,256]{2,1,0:T(8,128)(2,1)S(1)} custom-call(bf16[16,128,256]{2,1,0:T(8,128)(2,1)S(1)} %all-to-all-done.source, f32[17,128,512]{2,1,0:T(8,128)} %shard_map.185.response, f32[17,256]{1,0:T(8,128)S(1)} %copy-done.3, f32[17,256]{1,0:T(8,128)S(1)} %copy-done.2, f32[17,256]{1,0:T(8,128)S(1)} %copy-done.5, f32[17,256]{1,0:T(8,128)S(1)} %copy-done.4, ...), custom_call_target="tpu_custom_call" | custom-call | flops 2281701376 | bytes 128 | tf_op jit(solution)/shard_map/pallas_call | solution.py:513
  79.8 31.8 %all_to_all.15 = bf16[16,128,256]{2,1,0:T(8,128)(2,1)S(1)} all-to-all(bf16[16,128,256]{2,1,0:T(8,128)(2,1)S(1)} %shard_map.186), channel_id=1, replica_groups=mesh['ctx'=16,'ch'=2] {'ctx'}, dimensions={0} | all-to-all | bytes 2097152 | tf_op jit(solution)/shard_map/all_to_all | solution.py:583
  111.6 1.6 %fusion.1 = bf16[2048,256]{1,0:T(8,128)(2,1)} fusion(bf16[2048,256]{1,0:T(8,128)(2,1)S(1)} %copy-done.6, bf16[2048,256]{1,0:T(8,128)(2,1)S(1)} %copy-done.8, bf16[16,128,256]{2,1,0:T(8,128)(2,1)S(1)} %all_to_all.15, f32[2048]{0:T(1024)S(1)} %copy-done.9), kind=kLoop, calls=%fused_computation.2 | loop fusion | flops 3670016 | bytes 4202496 | tf_op jit(solution)/shard_map/convert_element_type | solution.py:652
  (22 shorter events, 0.1 us)
Async XLA Ops:
  4.4 11.0 %collective-permute-start.1 = (bf16[2048,128]{1,0:T(8,128)(2,1)}, bf16[2048,128]{1,0:T(8,128)(2,1)S(1)}, u32[]{:S(2)}, u32[]{:S(2)}) collective-permute-start(bf16[2048,128]{1,0:T(8,128)(2,1)} %get-tuple-element.12), channel_id=1, source_target_pairs={{0,2},{2,4},{4,6},{6,8},{8,10},{10,12},{12,14},{14,16},{16,18},{18... | collective-permute-start | bytes 1572872 | tf_op jit(solution)/shard_map/ppermute | solution.py:634
  8.9 21.2 %collective-permute-start = (bf16[2048,128]{1,0:T(8,128)(2,1)}, bf16[2048,128]{1,0:T(8,128)(2,1)S(1)}, u32[]{:S(2)}, u32[]{:S(2)}) collective-permute-start(bf16[2048,128]{1,0:T(8,128)(2,1)} %get-tuple-element.13.late), channel_id=1, source_target_pairs={{0,1},{1,0},{2,3},{3,2},{4,5},{5,4},{6,7},{7,6},{8,9},{9,8},{10,11... | collective-permute-start | bytes 1572872 | tf_op jit(solution)/shard_map/ppermute | solution.py:635
  10.2 33.0 %all-to-all-start.1 = ((bf16[16,128,256]{2,1,0:T(8,128)(2,1)}), bf16[16,128,256]{2,1,0:T(8,128)(2,1)S(1)}, u32[]{:S(2)}, u32[]{:S(2)}) async-start(bf16[16,128,256]{2,1,0:T(8,128)(2,1)} %bitcast.5), calls=%async_computation.1 | async-start | bytes 2097152 | tf_op jit(solution)/shard_map/all_to_all | solution.py:583
  15.4 0.8 copy-start.12
  20.5 13.8 %collective-permute-start.2 = (bf16[2048,128]{1,0:T(8,128)(2,1)}, bf16[2048,128]{1,0:T(8,128)(2,1)S(1)}, u32[]{:S(2)}, u32[]{:S(2)}) collective-permute-start(bf16[2048,128]{1,0:T(8,128)(2,1)} %shard_map.182.early), channel_id=1, source_target_pairs={{0,1},{1,0},{2,3},{3,2},{4,5},{5,4},{6,7},{7,6},{8,9},{9,8},{10,11... | collective-permute-start | bytes 1572872 | tf_op jit(solution)/shard_map/ppermute | solution.py:639
  30.1 4.2 %copy-start.10 = (bf16[2048,128]{1,0:T(8,128)(2,1)}, bf16[2048,128]{1,0:T(8,128)(2,1)S(1)}, u32[]{:S(2)}) copy-start(bf16[2048,128]{1,0:T(8,128)(2,1)S(1)} %collective-permute-done.late) | copy-start | bytes 1572868
  34.3 0.8 copy-start.11
  43.2 6.3 %copy-start.7 = (bf16[16,128,256]{2,1,0:T(8,128)(2,1)}, bf16[16,128,256]{2,1,0:T(8,128)(2,1)S(1)}, u32[]{:S(2)}) copy-start(bf16[16,128,256]{2,1,0:T(8,128)(2,1)S(1)} %all-to-all-done.1.source) | copy-start | bytes 3145732
  43.2 29.4 %all-to-all-start = ((bf16[16,128,256]{2,1,0:T(8,128)(2,1)}), bf16[16,128,256]{2,1,0:T(8,128)(2,1)S(1)}, u32[]{:S(2)}, u32[]{:S(2)}) async-start(bf16[16,128,256]{2,1,0:T(8,128)(2,1)} %bitcast.9), calls=%async_computation | async-start | bytes 2097152 | tf_op jit(solution)/shard_map/all_to_all | solution.py:583
  49.6 23.1 %copy-start = (bf16[512,512]{1,0:T(8,128)(2,1)S(1)}, bf16[512,512]{1,0:T(8,128)(2,1)}, u32[]{:S(2)}) copy-start(bf16[512,512]{1,0:T(8,128)(2,1)} %constant.62.clone.high.forward) | copy-start | bytes 1572868
  49.6 23.1 %copy-start.1 = (bf16[512,512]{1,0:T(8,128)(2,1)S(1)}, bf16[512,512]{1,0:T(8,128)(2,1)}, u32[]{:S(2)}) copy-start(bf16[512,512]{1,0:T(8,128)(2,1)} %constant.66.clone.inverse) | copy-start | bytes 1572868
  49.6 23.1 %copy-start.2 = (f32[17,256]{1,0:T(8,128)S(1)}, f32[17,256]{1,0:T(8,128)}, u32[]{:S(2)}) copy-start(f32[17,256]{1,0:T(8,128)} %constant.61.clone.turn_im) | copy-start | bytes 52228
  49.6 23.1 %copy-start.3 = (f32[17,256]{1,0:T(8,128)S(1)}, f32[17,256]{1,0:T(8,128)}, u32[]{:S(2)}) copy-start(f32[17,256]{1,0:T(8,128)} %constant.60.clone.turn_re) | copy-start | bytes 52228
  49.6 23.1 %copy-start.4 = (f32[17,256]{1,0:T(8,128)S(1)}, f32[17,256]{1,0:T(8,128)}, u32[]{:S(2)}) copy-start(f32[17,256]{1,0:T(8,128)} %constant.65.clone.back_im) | copy-start | bytes 52228
  49.6 23.1 %copy-start.5 = (f32[17,256]{1,0:T(8,128)S(1)}, f32[17,256]{1,0:T(8,128)}, u32[]{:S(2)}) copy-start(f32[17,256]{1,0:T(8,128)} %constant.64.clone.back_re) | copy-start | bytes 52228
  72.7 38.9 %copy-start.9 = (f32[2048]{0:T(1024)S(1)}, f32[2048]{0:T(1024)}, u32[]{:S(2)}) copy-start(f32[2048]{0:T(1024)} %param.27) | copy-start | bytes 24580
  79.8 31.8 %copy-start.6 = (bf16[2048,256]{1,0:T(8,128)(2,1)S(1)}, bf16[2048,256]{1,0:T(8,128)(2,1)}, u32[]{:S(2)}) copy-start(bf16[2048,256]{1,0:T(8,128)(2,1)} %shard_map.184) | copy-start | bytes 3145732
  79.8 31.8 %copy-start.8 = (bf16[2048,256]{1,0:T(8,128)(2,1)S(1)}, bf16[2048,256]{1,0:T(8,128)(2,1)}, u32[]{:S(2)}) copy-start(bf16[2048,256]{1,0:T(8,128)(2,1)} %param.24) | copy-start | bytes 3145732

commit v2 on v0

--- a/solution.py
+++ b/solution.py
@@ -39,14 +39,15 @@
     inverse = forward.T * (2.0 / size)
     inverse[0] /= 2.0
     inverse[half] /= 2.0
-    return split_table(forward) + split_table(inverse[:, half:])
-
-
-def short_filter(window, taps, query, fwd_hi, fwd_lo, inv_hi, inv_lo):
+    return (*split_table(forward), np.concatenate(split_table(inverse[:, half:]), axis=1))
+
+
+def short_filter(window, taps, query, fwd_hi, fwd_lo, inverse):
     half = taps.shape[1]
     spec = dot(window, fwd_hi) + dot(window, fwd_lo)
     taps_hi, taps_lo = split_value(taps)
-    resp = dot(taps_hi, fwd_hi[:half]) + dot(taps_lo, fwd_hi[:half]) + dot(taps_hi, fwd_lo[:half])
+    doubled = jnp.concatenate([fwd_hi[:half], fwd_hi[:half]], axis=0)
+    resp = dot(jnp.concatenate([taps_hi, taps_lo], axis=1), doubled) + dot(taps_hi, fwd_lo[:half])
     first = lax.broadcasted_iota(jnp.int32, (taps.shape[0], half), 1) == 0
     resp_re, resp_im = resp[:, :half], resp[:, half:]
     cross = jnp.where(first, 0.0, resp_im)
@@ -56,7 +57,8 @@
         [spec_re * resp_re - spec_im * cross, spec_re * cross + spec_im * own], axis=1
     )
     prod_hi, prod_lo = split_value(prod)
-    mixed = dot(prod_hi, inv_hi) + dot(prod_lo, inv_hi) + dot(prod_hi, inv_lo)
+    both = dot(prod_hi, inverse)
+    mixed = both[:, :half] + both[:, half:] + dot(prod_lo, inverse[:, :half])
     return (query.astype(F32) * mixed).astype(BF16)
 
 
@@ -64,17 +66,18 @@
     return (key.astype(F32) * value.astype(F32)).astype(BF16)
 
 
-def late_kernel(key, value, query, taps, fwd_hi, fwd_lo, inv_hi, inv_lo, out):
+def late_kernel(key, value, query, taps, fwd_hi, fwd_lo, inverse, out, border):
     window = gate_input(key[...], value[...])
+    border[...] = window[:, query.shape[1] :]
     out[...] = short_filter(
-        window, taps[...], query[...], fwd_hi[...], fwd_lo[...], inv_hi[...], inv_lo[...]
-    )
-
-
-def early_kernel(border, key, value, query, taps, fwd_hi, fwd_lo, inv_hi, inv_lo, out):
+        window, taps[...], query[...], fwd_hi[...], fwd_lo[...], inverse[...]
+    )
+
+
+def early_kernel(border, key, value, query, taps, fwd_hi, fwd_lo, inverse, out):
     window = jnp.concatenate([border[...], gate_input(key[...], value[...])], axis=1)
     out[...] = short_filter(
-        window, taps[...], query[...], fwd_hi[...], fwd_lo[...], inv_hi[...], inv_lo[...]
+        window, taps[...], query[...], fwd_hi[...], fwd_lo[...], inverse[...]
     )
 
 
@@ -82,69 +85,98 @@
     return pl.BlockSpec(array.shape, lambda *_: (0,) * array.ndim)
 
 
-def short_conv(border, key, value, query, taps, tables):
+def short_conv(border, key, value, query, taps, tables, block=1024):
     rows, tokens = key.shape
     half = tokens // 2
-    block = min(rows, 512)
+    block = min(rows, block)
     table_specs = [whole_spec(t) for t in tables]
     full = pl.BlockSpec((block, tokens), lambda i: (i, 0))
     left = pl.BlockSpec((block, half), lambda i: (i, 0))
     right = pl.BlockSpec((block, half), lambda i: (i, 1))
     if border is None:
-        body, specs, args = late_kernel, [full, full, right, left], (key, value, query, taps)
+        body, specs, outs = late_kernel, [full, full, right, left], 2
+        args = (key, value, query, taps)
     else:
-        body, specs = early_kernel, [left, left, left, left, left]
+        body, specs, outs = early_kernel, [left, left, left, left, left], 1
         args = (border, key, value, query, taps)
     return pl.pallas_call(
         body,
         grid=(rows // block,),
         in_specs=specs + table_specs,
-        out_specs=left,
-        out_shape=jax.ShapeDtypeStruct((rows, half), BF16),
-        compiler_params=pltpu.CompilerParams(vmem_limit_bytes=32 * MIB),
+        out_specs=[left] * outs,
+        out_shape=[jax.ShapeDtypeStruct((rows, half), BF16)] * outs,
+        compiler_params=pltpu.CompilerParams(vmem_limit_bytes=(60 if border is None else 48) * MIB),
         cost_estimate=pl.CostEstimate(
-            flops=10 * rows * tokens * tokens, bytes_accessed=8 * rows * tokens, transcendentals=0
+            flops=50 * rows * tokens * tokens, bytes_accessed=8 * rows * tokens, transcendentals=0
         ),
     )(*args, *tables)
 
 
-def own_kernel(which, weight, late, early, out):
+def own_kernel(which, weight, late, early, late_out, early_out):
     del which
-    out[...] = dot(weight[...], jnp.concatenate([early[...], late[...]], axis=1))
-
-
-def other_kernel(which, weight, late, early, total, key, out):
+    half = late.shape[1]
+    found = dot(weight[...], jnp.concatenate([late[...], early[...]], axis=1))
+    late_out[...] = found[:, :half]
+    early_out[...] = found[:, half:]
+
+
+def other_kernel(which, weight, piece, total, key, *refs):
     del which
-    values = total[...] + dot(weight[...], jnp.concatenate([early[...], late[...]], axis=1))
-    out[...] = (key[...].astype(F32) * values).astype(BF16)
-
-
-def project(which, weight, late, early, total=None, key=None):
-    rows, depth = weight.shape[0], late.shape[0]
-    half = late.shape[1]
-    block = min(rows, 256)
-    moving = pl.BlockSpec((block, 2 * half), lambda i, w: (i, 0))
+    values = total[...] + dot(weight[...], piece[...])
+    refs[-1][...] = (key[...].astype(F32) * values).astype(BF16)
+
+
+BLOCK = 1024
+
+
+def project_own(which, weight, late, early):
+    rows, (depth, half) = weight.shape[0], late.shape
+    block = min(rows, BLOCK)
+    whole = pl.BlockSpec((depth, half), lambda i, w: (0, 0))
+    moving = pl.BlockSpec((block, half), lambda i, w: (i, 0))
+    return pl.pallas_call(
+        own_kernel,
+        grid_spec=pltpu.PrefetchScalarGridSpec(
+            num_scalar_prefetch=1,
+            grid=(rows // block,),
+            in_specs=[pl.BlockSpec((block, depth), lambda i, w: (i, w[0])), whole, whole],
+            out_specs=[moving, moving],
+        ),
+        out_shape=[jax.ShapeDtypeStruct((rows, half), F32)] * 2,
+        compiler_params=pltpu.CompilerParams(vmem_limit_bytes=VMEM_PROJECT),
+        cost_estimate=pl.CostEstimate(
+            flops=4 * rows * depth * half, bytes_accessed=2 * rows * depth, transcendentals=0
+        ),
+    )(which, weight, late, early)
+
+
+VMEM_PROJECT = 46 * MIB
+
+
+def project_other(which, weight, piece, total, key, side, given=None):
+    rows, (depth, half) = weight.shape[0], piece.shape
+    block = min(rows, BLOCK)
+    at_side = pl.BlockSpec((block, half), lambda i, w: (i, side))
     specs = [
         pl.BlockSpec((block, depth), lambda i, w: (i, w[0])),
         pl.BlockSpec((depth, half), lambda i, w: (0, 0)),
-        pl.BlockSpec((depth, half), lambda i, w: (0, 0)),
+        pl.BlockSpec((block, half), lambda i, w: (i, 0)),
+        at_side,
     ]
-    args = [weight, late, early]
-    if total is None:
-        body, dtype = own_kernel, F32
-    else:
-        body, dtype = other_kernel, BF16
-        specs += [moving, moving]
-        args += [total, key]
+    args = [weight, piece, total, key]
+    if given is not None:
+        specs.append(pl.BlockSpec(memory_space=pl.ANY))
+        args.append(given)
     return pl.pallas_call(
-        body,
+        other_kernel,
         grid_spec=pltpu.PrefetchScalarGridSpec(
-            num_scalar_prefetch=1, grid=(rows // block,), in_specs=specs, out_specs=moving
-        ),
-        out_shape=jax.ShapeDtypeStruct((rows, 2 * half), dtype),
-        compiler_params=pltpu.CompilerParams(vmem_limit_bytes=32 * MIB),
+            num_scalar_prefetch=1, grid=(rows // block,), in_specs=specs, out_specs=at_side
+        ),
+        out_shape=jax.ShapeDtypeStruct((rows, 2 * half), BF16),
+        input_output_aliases={} if given is None else {5: 0},
+        compiler_params=pltpu.CompilerParams(vmem_limit_bytes=VMEM_PROJECT),
         cost_estimate=pl.CostEstimate(
-            flops=4 * rows * depth * half, bytes_accessed=2 * rows * depth, transcendentals=0
+            flops=16 * rows * depth * half, bytes_accessed=2 * rows * depth, transcendentals=0
         ),
     )(which, *args)
 
@@ -278,7 +310,7 @@
 SUBS = 16
 
 
-def forward_slabs(source, turn_re, turn_im, high, low):
+def forward_slabs(source, turn_re, turn_im, parts):
     slabs, rows, tokens = source.shape
     lanes = min(tokens, LANES)
     subs = min(rows, SUBS)
@@ -296,50 +328,55 @@
                     out = (re * cos - im * sin, re * sin + im * cos)
                 for part, value in enumerate(out):
                     where = slice(part * tokens + lane, part * tokens + lane + lanes)
-                    hi, lo = split_value(value)
-                    high[k, at, where] = hi
-                    low[k, at, where] = lo
+                    store_split(parts, (k, at, where), value)
             return carry
 
         lax.fori_loop(0, rows // subs, tile, 0)
 
 
-def product3(high, low, table_hi, table_lo):
-    a, b = high[...], low[...]
-    shape = a.shape
-    a = a.reshape(shape[0] * shape[1], shape[2])
-    b = b.reshape(shape[0] * shape[1], shape[2])
-    out = dot(a, table_hi[...]) + dot(b, table_hi[...]) + dot(a, table_lo[...])
-    return out.reshape(shape[0], shape[1], -1)
-
-
-def response_kernel(source, turn_re, turn_im, table_hi, table_lo, out, high, low):
-    forward_slabs(source, turn_re, turn_im, high, low)
-    out[...] = product3(high, low, table_hi, table_lo)
-
-
-def convolve_kernel(
-    source, response, turn_re, turn_im, back_re, back_im, fwd_hi, fwd_lo, inv_hi, inv_lo, out, high, low, spec
-):
-    slabs, rows, tokens = source.shape
-    lanes = min(tokens, LANES)
-    subs = min(rows, SUBS)
-    forward_slabs(source, turn_re, turn_im, high, low)
-    spec[...] = product3(high, low, fwd_hi, fwd_lo)
-
-    def multiply(k, carry):
+def store_split(parts, where, value):
+    high = value.astype(BF16)
+    parts[0][where] = high
+    if len(parts) > 1:
+        parts[1][where] = (value - high.astype(F32)).astype(BF16)
+
+
+def product(parts, tables):
+    slabs, rows, depth = parts[0].shape
+    flat = [p[...].reshape(slabs * rows, depth) for p in parts]
+    out = dot(flat[0], tables[0][...])
+    for left, right in zip(flat[1:], tables):
+        out += dot(left, right[...])
+    for right in tables[1:]:
+        out += dot(flat[0], right[...])
+    return out.reshape(slabs, rows, depth)
+
+
+def response_kernel(source, turn_re, turn_im, high, low, out, *parts):
+    forward_slabs(source, turn_re, turn_im, parts)
+    out[...] = product(parts, (high, low))
+
+
+def multiply(spec, response, parts):
+    tokens = spec.shape[2] // 2
+
+    def one(k, carry):
         sig_re, sig_im = spec[k, :, :tokens], spec[k, :, tokens:]
         res_re, res_im = response[k, :, :tokens], response[k, :, tokens:]
         for part, value in enumerate(
             (sig_re * res_re - sig_im * res_im, sig_re * res_im + sig_im * res_re)
         ):
-            hi, lo = split_value(value)
-            high[k, :, part * tokens : (part + 1) * tokens] = hi
-            low[k, :, part * tokens : (part + 1) * tokens] = lo
+            where = (k, slice(None), slice(part * tokens, (part + 1) * tokens))
+            store_split(parts, where, value)
         return carry
 
-    lax.fori_loop(0, slabs + 1, multiply, 0)
-    spec[...] = product3(high, low, inv_hi, inv_lo)
+    lax.fori_loop(0, spec.shape[0], one, 0)
+
+
+def back_slabs(spec, back_re, back_im, out):
+    slabs, rows, tokens = out.shape
+    lanes = min(tokens, LANES)
+    subs = min(rows, SUBS)
     for lane in range(0, tokens, lanes):
 
         def tile(step, carry, lane=lane):
@@ -361,36 +398,67 @@
         lax.fori_loop(0, rows // subs, tile, 0)
 
 
-def long_call(source, response, tables, start=0, count=None):
+def convolve_kernel(
+    block, source, response, turn_re, turn_im, back_re, back_im, forward, inverse, out, spec, part, held, sem
+):
+    copies = []
+    for i in range(source.shape[1] // block):
+        rows = pl.ds(i * block, block)
+        copies.append(pltpu.make_async_copy(response.at[:, rows, :], held.at[i], sem.at[i]))
+        copies[-1].start()
+    for i, copy in enumerate(copies):
+        rows = pl.ds(i * block, block)
+        forward_slabs(source.at[:, rows, :], turn_re, turn_im, [part])
+        spec[...] = product([part], (forward,))
+        copy.wait()
+        multiply(spec, held.at[i], [part])
+        spec[...] = product([part], (inverse,))
+        back_slabs(spec, back_re, back_im, out.at[:, rows, :])
+
+
+def convolve_call(source, response, tables, block=64):
     slabs, rows, tokens = source.shape
-    block = min(rows, 32)
+    block = min(rows, block)
     turns, forward, inverse = tables
-    if response is None:
-        body, given = response_kernel, [*turns[:2], *forward]
-    else:
-        body, given = convolve_kernel, [*turns, *forward, *inverse]
-    data = pl.BlockSpec((slabs, block, tokens), lambda i: (0, i, 0))
-    wide = pl.BlockSpec((slabs + 1, block, 2 * tokens), lambda i: (0, i, 0))
-    scratch = [pltpu.VMEM((slabs + 1, block, 2 * tokens), t) for t in (BF16, BF16, F32)]
-    flops = 12 * (slabs + 1) * rows * 4 * tokens * tokens
-    if response is None:
-        out_spec, out_shape, scratch = wide, ((slabs + 1, rows, 2 * tokens), F32), scratch[:2]
-        args, specs = [source], [data]
-    else:
-        out_spec, out_shape = data, ((slabs, rows, tokens), BF16)
-        args, specs = [source, response], [data, wide]
+    here = pl.BlockSpec(memory_space=pltpu.VMEM)
+    wide = (slabs + 1, block, 2 * tokens)
     return pl.pallas_call(
-        body,
-        grid=(rows // block,),
-        in_specs=specs + [whole_spec(t) for t in given],
-        out_specs=out_spec,
-        out_shape=jax.ShapeDtypeStruct(*out_shape),
-        scratch_shapes=scratch,
+        functools.partial(convolve_kernel, block),
+        in_specs=[here, pl.BlockSpec(memory_space=pl.ANY)] + [here] * 6,
+        out_specs=here,
+        out_shape=jax.ShapeDtypeStruct((slabs, rows, tokens), BF16),
+        scratch_shapes=[
+            pltpu.VMEM(wide, F32),
+            pltpu.VMEM(wide, BF16),
+            pltpu.VMEM((rows // block, *wide), F32),
+            pltpu.SemaphoreType.DMA((rows // block,)),
+        ],
         compiler_params=pltpu.CompilerParams(vmem_limit_bytes=48 * MIB),
         cost_estimate=pl.CostEstimate(
-            flops=flops, bytes_accessed=8 * (slabs + 1) * rows * tokens, transcendentals=0
-        ),
-    )(*args, *given)
+            flops=16 * (slabs + 1) * rows * tokens * tokens, bytes_accessed=rows, transcendentals=0
+        ),
+    )(source, response, *turns, forward[0], inverse[0])
+
+
+def response_call(source, tables, block=32):
+    slabs, rows, tokens = source.shape
+    block = min(rows, block)
+    turns, forward, _ = tables
+    given = [*turns[:2], *forward]
+    wide = (slabs + 1, block, 2 * tokens)
+    return pl.pallas_call(
+        response_kernel,
+        grid=(rows // block,),
+        in_specs=[pl.BlockSpec((slabs, block, tokens), lambda i: (0, i, 0))]
+        + [whole_spec(t) for t in given],
+        out_specs=pl.BlockSpec(wide, lambda i: (0, i, 0)),
+        out_shape=jax.ShapeDtypeStruct((slabs + 1, rows, 2 * tokens), F32),
+        scratch_shapes=[pltpu.VMEM(wide, BF16)] * 2,
+        compiler_params=pltpu.CompilerParams(vmem_limit_bytes=60 * MIB),
+        cost_estimate=pl.CostEstimate(
+            flops=24 * (slabs + 1) * rows * tokens * tokens, bytes_accessed=rows, transcendentals=0
+        ),
+    )(source, *given)
 
 
 def exchange(value, groups):
@@ -409,26 +477,25 @@
     short = short_tables(tokens)
     tables = long_tables(groups, tokens)
     swap = [(0, 1), (1, 0)]
-
-    border = gate_input(mr_key[:, half:], mr_value[:, half:])
+    mine = lax.axis_index("ch").astype(jnp.int32).reshape(1)
+
+    late, border = short_conv(None, mr_key, mr_value, mr_query, mr_filter, short)
     border = lax.ppermute(border, "ctx", [(i, i + 1) for i in range(groups - 1)])
+    other_late = lax.ppermute(late, "ch", swap)
+    li_filter, late = lax.optimization_barrier((li_filter, late))
     filter_part = exchange(li_filter, groups)
-
-    late = short_conv(None, mr_key, mr_value, mr_query, mr_filter, short)
-    other_late = lax.ppermute(late, "ch", swap)
-    early = short_conv(border, mr_key, mr_value, mr_query, mr_filter, short)
+    (early,) = short_conv(border, mr_key, mr_value, mr_query, mr_filter, short)
     other_early = lax.ppermute(early, "ch", swap)
 
-    me = lax.axis_index("ch").astype(jnp.int32).reshape(1)
-    total = project(me, proj_weight, late, early)
-    li_input = project(1 - me, proj_weight, other_late, other_early, total, li_key)
-
-    response = long_call(filter_part, None, tables)
-    long_part = long_call(exchange(li_input, groups), response, tables)
+    late_total, early_total = project_own(mine, proj_weight, late, early)
+    li_input = project_other(1 - mine, proj_weight, other_late, late_total, li_key, 1)
+    li_input = project_other(1 - mine, proj_weight, other_early, early_total, li_key, 0, li_input)
+
+    direct = li_skip[:, None] * li_input.astype(F32)
+    response, direct = lax.optimization_barrier((response_call(filter_part, tables), direct))
+    long_part = convolve_call(exchange(li_input, groups), response, tables)
     long_local = exchange(long_part.reshape(rows, tokens), groups).reshape(rows, tokens)
-    gated_out = li_query.astype(F32) * (
-        long_local.astype(F32) + li_skip[:, None] * li_input.astype(F32)
-    )
+    gated_out = li_query.astype(F32) * (long_local.astype(F32) + direct)
     return gated_out.astype(BF16)
 
 

time: 146 us -> 110 us (0.75)
  starting transfers between devices: 32.3 us -> 18.5 us
  local copies, waits for them, and re-layouts: 12.9 us -> 1.3 us
  waiting for transfers between devices: 20.1 us -> 13.7 us
  Pallas kernels: 45.5 us -> 39.1 us
  other arithmetic: 2.91 us -> 4.47 us
    all_to_all x2, starting transfers between devices: 26.3 us -> 11.3 us  [exchange(): lax.all_to_all(value.reshape(groups, rows // groups, tokens), 'ctx', spli...]
    unnamed x42 -> x36, local copies, waits for them, and re-layouts: 12.9 us -> 1.3 us
    ppermute x1, waiting for transfers between devices: 5.31 us -> 0.12 us  [on_device(): lax.ppermute(border, 'ctx', [(i, i + 1) for i in range(groups - 1)])]
    all_to_all x2, waiting for transfers between devices: 14.7 us -> 11.4 us  [exchange(): lax.all_to_all(value.reshape(groups, rows // groups, tokens), 'ctx', spli...]
    pallas_call x2, Pallas kernels: 10.7 us -> 7.44 us  [short_conv(): pl.pallas_call(body, grid=(rows // block,), in_specs=specs + table_specs,...]
    pallas_call x4 -> x5, Pallas kernels: 34.8 us -> 31.6 us  [the longest x2 11.1 us: project_other(): pl.pallas_call(other_kernel, grid_spec=pltpu.PrefetchScalarGridSpec(num_s...]
    mul x0 -> x1, other arithmetic: none -> 2.96 us  [on_device(): direct = li_skip[:, None] * li_input.astype(F32)]
    ppermute x1, waiting for transfers between devices: 0.08 us -> 2.16 us  [on_device(): other_early = lax.ppermute(early, 'ch', swap)]
  transfers between devices with their start and end apart: 5 -> 5, of which waited for: 3 -> 3; matrix products, arithmetic and copies ran while one was open for 0% -> 3% of each run, Pallas kernels for 21% -> 25%
where the time goes in v2:
time: 110 us; the launch traced here: 109 us
  Pallas kernels  39.1 us (36%)
  blocking collectives  31.8 us (29%)
  starting transfers between devices  18.5 us (17%)
  waiting for transfers between devices  13.7 us (12%)
  other arithmetic  4.47 us (4%)
  local copies, waits for them, and re-layouts  1.3 us (1%)
    all_to_all x1, blocking collectives, exchange(): lax.all_to_all(value.reshape(groups, rows // groups, tokens), 'ctx', spli...  31.8 us
    all_to_all x2, waiting for transfers between devices, exchange(): lax.all_to_all(value.reshape(groups, rows // groups, tokens), 'ctx', spli...  11.4 us
    all_to_all x2, starting transfers between devices, exchange(): lax.all_to_all(value.reshape(groups, rows // groups, tokens), 'ctx', spli...  11.3 us
    pallas_call x2, Pallas kernels, project_other(): pl.pallas_call(other_kernel, grid_spec=pltpu.PrefetchScalarGridSpec(num_s...  11.1 us
    pallas_call x1, Pallas kernels, response_call(): pl.pallas_call(response_kernel, grid=(rows // block,), in_specs=[pl.Block...  8.71 us
    pallas_call x2, Pallas kernels, short_conv(): pl.pallas_call(body, grid=(rows // block,), in_specs=specs + table_specs,...  7.44 us
    pallas_call x1, Pallas kernels, convolve_call(): pl.pallas_call(functools.partial(convolve_kernel, block), in_specs=[here,...  7.12 us
    pallas_call x1, Pallas kernels, project_own(): pl.pallas_call(own_kernel, grid_spec=pltpu.PrefetchScalarGridSpec(num_sca...  4.74 us
  transfers between devices with their start and end apart: 5, of which 3 were waited for; matrix products, arithmetic and copies ran while one was open for 3% of the time, Pallas kernels for 25%

profile of v2, /device:TPU:1, one launch (start us, length us, event | category | flops | bytes accessed | tf_op | source)
XLA Modules:
  0.0 109.1 jit_solution(6334427018117012875)
XLA Ops:
  0.0 0.0 copy-start.10
  0.0 4.5 %shard_map.181 = (bf16[2048,128]{1,0:T(8,128)(2,1)}, bf16[2048,128]{1,0:T(8,128)(2,1)}) custom-call(bf16[2048,256]{1,0:T(8,128)(2,1)} %key.5, bf16[2048,256]{1,0:T(8,128)(2,1)} %value.3, bf16[2048,256]{1,0:T(8,128)(2,1)} %query.3, f32[2048,128]{1,0:T(8,128)} %taps.3, bf16[256,256]{1,0:T(8,128)(2,1)} %constant.26.clone.fwd_hi, ...), custom_call_target="tpu_custom_call" | custom-call | flops 6710886400 | bytes 4194304 | tf_op jit(solution)/shard_map/pallas_call | solution.py:102
  4.6 4.7 %collective-permute-start = (bf16[2048,128]{1,0:T(8,128)(2,1)}, bf16[2048,128]{1,0:T(8,128)(2,1)}, u32[]{:S(2)}, u32[]{:S(2)}) collective-permute-start(bf16[2048,128]{1,0:T(8,128)(2,1)} %get-tuple-element.13), channel_id=1, source_target_pairs={{0,2},{2,4},{4,6},{6,8},{8,10},{10,12},{12,14},{14,16},{16,18},{18... | collective-permute-start | bytes 1572872 | tf_op jit(solution)/shard_map/ppermute | solution.py:483
  9.2 1.3 %collective-permute-start.2 = (bf16[2048,128]{1,0:T(8,128)(2,1)}, bf16[2048,128]{1,0:T(8,128)(2,1)}, u32[]{:S(2)}, u32[]{:S(2)}) collective-permute-start(bf16[2048,128]{1,0:T(8,128)(2,1)} %get-tuple-element.15.late), channel_id=1, source_target_pairs={{0,1},{1,0},{2,3},{3,2},{4,5},{5,4},{6,7},{7,6},{8,9},{9,8},{10,11... | collective-permute-start | bytes 1572872 | tf_op jit(solution)/shard_map/ppermute | solution.py:484
  10.5 5.0 %all-to-all-start.1 = ((bf16[16,128,256]{2,1,0:T(8,128)(2,1)}), bf16[16,128,256]{2,1,0:T(8,128)(2,1)}, u32[]{:S(2)}, u32[]{:S(2)}) async-start(bf16[16,128,256]{2,1,0:T(8,128)(2,1)} %bitcast.6), calls=%async_computation.1 | async-start | bytes 2097152 | tf_op jit(solution)/shard_map/all_to_all | solution.py:466
  15.5 0.1 collective-permute-done.border
  15.7 1.2 %copy-done.4 = f32[2048,128]{1,0:T(8,128)S(1)} copy-done((f32[2048,128]{1,0:T(8,128)S(1)}, f32[2048,128]{1,0:T(8,128)}, u32[]{:S(2)}) %copy-start.4) | copy-done | bytes 1048600
  16.9 2.9 %shard_map.182.early = bf16[2048,128]{1,0:T(8,128)(2,1)S(1)} custom-call(bf16[2048,128]{1,0:T(8,128)(2,1)} %collective-permute-done.border, bf16[2048,256]{1,0:T(8,128)(2,1)S(1)} %copy-done.1, bf16[2048,256]{1,0:T(8,128)(2,1)S(1)} %copy-done.2, bf16[2048,256]{1,0:T(8,128)(2,1)S(1)} %copy-done.3, f32[2048,128]{1,0:T(8,128)S(1)} %copy-done.4, ...), custom_call_target="tpu_custom_call" | custom-call | flops 6710886400 | bytes 4194304 | tf_op jit(solution)/shard_map/pallas_call | solution.py:102
  19.8 0.0 copy-start.5
  19.9 1.3 %collective-permute-start.1 = (bf16[2048,128]{1,0:T(8,128)(2,1)S(1)}, bf16[2048,128]{1,0:T(8,128)(2,1)S(1)}, u32[]{:S(2)}, u32[]{:S(2)}) collective-permute-start(bf16[2048,128]{1,0:T(8,128)(2,1)S(1)} %shard_map.182.early), channel_id=1, source_target_pairs={{0,1},{1,0},{2,3},{3,2},{4,5},{5,4},{6,7},{7,6},{8,9},{9,8},{10,11... | collective-permute-start | bytes 1572872 | tf_op jit(solution)/shard_map/ppermute | solution.py:488
  21.1 4.7 %shard_map.183 = (f32[2048,128]{1,0:T(8,128)S(1)}, f32[2048,128]{1,0:T(8,128)S(1)}) custom-call(s32[1]{0:T(128)} %bitcast.which, bf16[2048,4096]{1,0:T(8,128)(2,1)} %weight.5, bf16[2048,128]{1,0:T(8,128)(2,1)S(1)} %copy-done, bf16[2048,128]{1,0:T(8,128)(2,1)S(1)} %shard_map.182.early), custom_call_target="tpu_custom_call" | custom-call | flops 2147483648 | bytes 8388608 | tf_op jit(solution)/shard_map/pallas_call | solution.py:137
  25.9 5.6 %shard_map.184.refs_0_ = bf16[2048,256]{1,0:T(8,128)(2,1)} custom-call(s32[1]{0:T(128)S(6)} %sub.4.which, bf16[2048,4096]{1,0:T(8,128)(2,1)} %weight.5, bf16[2048,128]{1,0:T(8,128)(2,1)} %collective-permute-done.2.piece, f32[2048,128]{1,0:T(8,128)S(1)} %get-tuple-element.17.total, bf16[2048,256]{1,0:T(8,128)(2,1)S(1)} %copy-done.5), custom_call_target="tpu_custom_call" | custom-call | flops 8589934592 | bytes 8388608 | tf_op jit(solution)/shard_map/pallas_call | solution.py:170
  31.5 2.2 %collective-permute-done.1.piece = bf16[2048,128]{1,0:T(8,128)(2,1)S(1)} collective-permute-done((bf16[2048,128]{1,0:T(8,128)(2,1)S(1)}, bf16[2048,128]{1,0:T(8,128)(2,1)S(1)}, u32[]{:S(2)}, u32[]{:S(2)}) %collective-permute-start.1) | collective-permute-done | bytes 524320 | tf_op jit(solution)/shard_map/ppermute | solution.py:488
  33.7 5.4 %shard_map.185 = bf16[2048,256]{1,0:T(8,128)(2,1)} custom-call(s32[1]{0:T(128)S(6)} %sub.4.which, bf16[2048,4096]{1,0:T(8,128)(2,1)} %weight.5, bf16[2048,128]{1,0:T(8,128)(2,1)S(1)} %collective-permute-done.1.piece, f32[2048,128]{1,0:T(8,128)S(1)} %get-tuple-element.16.total, bf16[2048,256]{1,0:T(8,128)(2,1)S(1)} %copy-done.5, ...), custom_call_target="tpu_custom_call", output_to_operand_aliasing={{}: (5, {})} | custom-call | flops 8589934592 | bytes 8388608 | tf_op jit(solution)/shard_map/pallas_call | solution.py:170
  39.2 6.3 %all-to-all-start = ((bf16[16,128,256]{2,1,0:T(8,128)(2,1)}), bf16[16,128,256]{2,1,0:T(8,128)(2,1)S(1)}, u32[]{:S(2)}, u32[]{:S(2)}) async-start(bf16[16,128,256]{2,1,0:T(8,128)(2,1)} %bitcast.1), calls=%async_computation | async-start | bytes 2097152 | tf_op jit(solution)/shard_map/all_to_all | solution.py:466
  45.5 3.0 %convert_multiply_fusion = f32[2048,256]{1,0:T(8,128)} fusion(bf16[2048,256]{1,0:T(8,128)(2,1)} %shard_map.185, f32[2048]{0:T(1024)S(1)} %copy-done.17), kind=kLoop, calls=%fused_computation.3 | loop fusion | flops 1048576 | bytes 3153920 | tf_op jit(solution)/shard_map/mul | solution.py:494
  48.4 0.0 copy-start.13
  48.4 0.0 copy-start.14
  48.5 8.7 %shard_map.186.response = f32[17,128,512]{2,1,0:T(8,128)} custom-call(bf16[16,128,256]{2,1,0:T(8,128)(2,1)} %all-to-all-done.1.source, f32[17,256]{1,0:T(8,128)} %constant.29.clone.turn_re, f32[17,256]{1,0:T(8,128)} %constant.30.clone.turn_im, bf16[512,512]{1,0:T(8,128)(2,1)} %constant.31.clone.high.forward, bf16[512,512]{1,0:T(8,128)(2,1)} %constant.32.clone.low), custom_call_target="tpu_custom_call" | custom-call | flops 3422552064 | bytes 128 | tf_op jit(solution)/shard_map/pallas_call | solution.py:449
  57.2 11.4 %all-to-all-done.source = bf16[16,128,256]{2,1,0:T(8,128)(2,1)S(1)} async-done(((bf16[16,128,256]{2,1,0:T(8,128)(2,1)}), bf16[16,128,256]{2,1,0:T(8,128)(2,1)S(1)}, u32[]{:S(2)}, u32[]{:S(2)}) %all-to-all-start) | async-done | bytes 1048608 | tf_op jit(solution)/shard_map/all_to_all | solution.py:466
  68.6 0.0 copy-start.16
  68.6 7.1 %shard_map.187 = bf16[16,128,256]{2,1,0:T(8,128)(2,1)S(1)} custom-call(bf16[16,128,256]{2,1,0:T(8,128)(2,1)S(1)} %all-to-all-done.source, f32[17,128,512]{2,1,0:T(8,128)} %shard_map.186.response, f32[17,256]{1,0:T(8,128)S(1)} %copy-done.12, f32[17,256]{1,0:T(8,128)S(1)} %copy-done.11, f32[17,256]{1,0:T(8,128)S(1)} %copy-done.14, f32[17,256]{1,0:T(8,128)S(1)} %copy-done.13, ...), custom_call_target="tpu_custom_call" | custom-call | flops 2281701376 | bytes 128 | tf_op jit(solution)/shard_map/pallas_call | solution.py:425
  75.8 31.8 %all_to_all.15 = bf16[16,128,256]{2,1,0:T(8,128)(2,1)S(1)} all-to-all(bf16[16,128,256]{2,1,0:T(8,128)(2,1)S(1)} %shard_map.187), channel_id=1, replica_groups=mesh['ctx'=16,'ch'=2] {'ctx'}, dimensions={0} | all-to-all | bytes 2097152 | tf_op jit(solution)/shard_map/all_to_all | solution.py:466
  107.6 1.5 %fusion.1 = bf16[2048,256]{1,0:T(8,128)(2,1)} fusion(f32[2048,256]{1,0:T(8,128)S(1)} %copy-done.15, bf16[2048,256]{1,0:T(8,128)(2,1)S(1)} %copy-done.16, bf16[16,128,256]{2,1,0:T(8,128)(2,1)S(1)} %all_to_all.15), kind=kLoop, calls=%fused_computation.2 | loop fusion | flops 2621440 | bytes 5242880 | tf_op jit(solution)/shard_map/convert_element_type | solution.py:499
  (32 shorter events, 0.1 us)
Async XLA Ops:
  0.0 15.7 %copy-start.3 = (bf16[2048,256]{1,0:T(8,128)(2,1)S(1)}, bf16[2048,256]{1,0:T(8,128)(2,1)}, u32[]{:S(2)}) copy-start(bf16[2048,256]{1,0:T(8,128)(2,1)} %query.3) | copy-start | bytes 3145732
  0.0 15.7 %copy-start.8 = (bf16[256,256]{1,0:T(8,128)(2,1)S(1)}, bf16[256,256]{1,0:T(8,128)(2,1)}, u32[]{:S(2)}) copy-start(bf16[256,256]{1,0:T(8,128)(2,1)} %constant.28.clone.inverse) | copy-start | bytes 393220
  0.0 15.7 %copy-start.9 = (bf16[256,256]{1,0:T(8,128)(2,1)S(1)}, bf16[256,256]{1,0:T(8,128)(2,1)}, u32[]{:S(2)}) copy-start(bf16[256,256]{1,0:T(8,128)(2,1)} %constant.27.clone.fwd_lo) | copy-start | bytes 393220
  0.0 15.7 %copy-start.10 = (bf16[256,256]{1,0:T(8,128)(2,1)S(1)}, bf16[256,256]{1,0:T(8,128)(2,1)}, u32[]{:S(2)}) copy-start(bf16[256,256]{1,0:T(8,128)(2,1)} %constant.26.clone.fwd_hi) | copy-start | bytes 393220
  4.5 11.1 %copy-start.1 = (bf16[2048,256]{1,0:T(8,128)(2,1)S(1)}, bf16[2048,256]{1,0:T(8,128)(2,1)}, u32[]{:S(2)}) copy-start(bf16[2048,256]{1,0:T(8,128)(2,1)} %key.5) | copy-start | bytes 3145732
  4.5 11.1 %copy-start.2 = (bf16[2048,256]{1,0:T(8,128)(2,1)S(1)}, bf16[2048,256]{1,0:T(8,128)(2,1)}, u32[]{:S(2)}) copy-start(bf16[2048,256]{1,0:T(8,128)(2,1)} %value.3) | copy-start | bytes 3145732
  4.6 11.1 %collective-permute-start = (bf16[2048,128]{1,0:T(8,128)(2,1)}, bf16[2048,128]{1,0:T(8,128)(2,1)}, u32[]{:S(2)}, u32[]{:S(2)}) collective-permute-start(bf16[2048,128]{1,0:T(8,128)(2,1)} %get-tuple-element.13), channel_id=1, source_target_pairs={{0,2},{2,4},{4,6},{6,8},{8,10},{10,12},{12,14},{14,16},{16,18},{18... | collective-permute-start | bytes 1572872 | tf_op jit(solution)/shard_map/ppermute | solution.py:483
  9.2 16.6 %collective-permute-start.2 = (bf16[2048,128]{1,0:T(8,128)(2,1)}, bf16[2048,128]{1,0:T(8,128)(2,1)}, u32[]{:S(2)}, u32[]{:S(2)}) collective-permute-start(bf16[2048,128]{1,0:T(8,128)(2,1)} %get-tuple-element.15.late), channel_id=1, source_target_pairs={{0,1},{1,0},{2,3},{3,2},{4,5},{5,4},{6,7},{7,6},{8,9},{9,8},{10,11... | collective-permute-start | bytes 1572872 | tf_op jit(solution)/shard_map/ppermute | solution.py:484
  10.5 28.6 %all-to-all-start.1 = ((bf16[16,128,256]{2,1,0:T(8,128)(2,1)}), bf16[16,128,256]{2,1,0:T(8,128)(2,1)}, u32[]{:S(2)}, u32[]{:S(2)}) async-start(bf16[16,128,256]{2,1,0:T(8,128)(2,1)} %bitcast.6), calls=%async_computation.1 | async-start | bytes 2097152 | tf_op jit(solution)/shard_map/all_to_all | solution.py:466
  15.5 5.6 %copy-start = (bf16[2048,128]{1,0:T(8,128)(2,1)S(1)}, bf16[2048,128]{1,0:T(8,128)(2,1)}, u32[]{:S(2)}) copy-start(bf16[2048,128]{1,0:T(8,128)(2,1)} %get-tuple-element.15.late) | copy-start | bytes 1572868
  15.7 1.2 %copy-start.4 = (f32[2048,128]{1,0:T(8,128)S(1)}, f32[2048,128]{1,0:T(8,128)}, u32[]{:S(2)}) copy-start(f32[2048,128]{1,0:T(8,128)} %taps.3) | copy-start | bytes 3145732
  19.8 6.0 %copy-start.5 = (bf16[2048,256]{1,0:T(8,128)(2,1)S(1)}, bf16[2048,256]{1,0:T(8,128)(2,1)}, u32[]{:S(2)}) copy-start(bf16[2048,256]{1,0:T(8,128)(2,1)} %key.7) | copy-start | bytes 3145732
  19.9 13.8 %collective-permute-start.1 = (bf16[2048,128]{1,0:T(8,128)(2,1)S(1)}, bf16[2048,128]{1,0:T(8,128)(2,1)S(1)}, u32[]{:S(2)}, u32[]{:S(2)}) collective-permute-start(bf16[2048,128]{1,0:T(8,128)(2,1)S(1)} %shard_map.182.early), channel_id=1, source_target_pairs={{0,1},{1,0},{2,3},{3,2},{4,5},{5,4},{6,7},{7,6},{8,9},{9,8},{10,11... | collective-permute-start | bytes 1572872 | tf_op jit(solution)/shard_map/ppermute | solution.py:488
  39.1 6.3 %copy-start.17 = (f32[2048]{0:T(1024)S(1)}, f32[2048]{0:T(1024)}, u32[]{:S(2)}) copy-start(f32[2048]{0:T(1024)} %param.27) | copy-start | bytes 24580
  39.2 29.4 %all-to-all-start = ((bf16[16,128,256]{2,1,0:T(8,128)(2,1)}), bf16[16,128,256]{2,1,0:T(8,128)(2,1)S(1)}, u32[]{:S(2)}, u32[]{:S(2)}) async-start(bf16[16,128,256]{2,1,0:T(8,128)(2,1)} %bitcast.1), calls=%async_computation | async-start | bytes 2097152 | tf_op jit(solution)/shard_map/all_to_all | solution.py:466
  48.4 20.2 %copy-start.6 = (bf16[512,512]{1,0:T(8,128)(2,1)S(1)}, bf16[512,512]{1,0:T(8,128)(2,1)}, u32[]{:S(2)}) copy-start(bf16[512,512]{1,0:T(8,128)(2,1)} %constant.31.clone.high.forward) | copy-start | bytes 1572868
  48.4 20.2 %copy-start.7 = (bf16[512,512]{1,0:T(8,128)(2,1)S(1)}, bf16[512,512]{1,0:T(8,128)(2,1)}, u32[]{:S(2)}) copy-start(bf16[512,512]{1,0:T(8,128)(2,1)} %constant.35.clone.inverse) | copy-start | bytes 1572868
  48.4 20.2 %copy-start.11 = (f32[17,256]{1,0:T(8,128)S(1)}, f32[17,256]{1,0:T(8,128)}, u32[]{:S(2)}) copy-start(f32[17,256]{1,0:T(8,128)} %constant.30.clone.turn_im) | copy-start | bytes 52228
  48.4 20.2 %copy-start.12 = (f32[17,256]{1,0:T(8,128)S(1)}, f32[17,256]{1,0:T(8,128)}, u32[]{:S(2)}) copy-start(f32[17,256]{1,0:T(8,128)} %constant.29.clone.turn_re) | copy-start | bytes 52228
  48.4 20.2 %copy-start.13 = (f32[17,256]{1,0:T(8,128)S(1)}, f32[17,256]{1,0:T(8,128)}, u32[]{:S(2)}) copy-start(f32[17,256]{1,0:T(8,128)} %constant.34.clone.back_im) | copy-start | bytes 52228
  48.4 20.2 %copy-start.14 = (f32[17,256]{1,0:T(8,128)S(1)}, f32[17,256]{1,0:T(8,128)}, u32[]{:S(2)}) copy-start(f32[17,256]{1,0:T(8,128)} %constant.33.clone.back_re) | copy-start | bytes 52228
  68.6 39.0 %copy-start.16 = (bf16[2048,256]{1,0:T(8,128)(2,1)S(1)}, bf16[2048,256]{1,0:T(8,128)(2,1)}, u32[]{:S(2)}) copy-start(bf16[2048,256]{1,0:T(8,128)(2,1)} %param.24) | copy-start | bytes 3145732
  75.8 31.8 %copy-start.15 = (f32[2048,256]{1,0:T(8,128)S(1)}, f32[2048,256]{1,0:T(8,128)}, u32[]{:S(2)}) copy-start(f32[2048,256]{1,0:T(8,128)} %convert_multiply_fusion) | copy-start | bytes 6291460

commit v3 on v2

--- a/solution.py
+++ b/solution.py
@@ -307,7 +307,7 @@
 
 
 LANES = 128
-SUBS = 16
+SUBS = 32
 
 
 def forward_slabs(source, turn_re, turn_im, parts):
@@ -416,7 +416,7 @@
         back_slabs(spec, back_re, back_im, out.at[:, rows, :])
 
 
-def convolve_call(source, response, tables, block=64):
+def convolve_call(source, response, tables, block=128):
     slabs, rows, tokens = source.shape
     block = min(rows, block)
     turns, forward, inverse = tables

time: 110 us -> 109 us (level)
  Pallas kernels: 39.1 us -> 37.7 us
where the time goes in v3:
time: 109 us; the launch traced here: 108 us
  Pallas kernels  37.7 us (35%)
  blocking collectives  31.8 us (29%)
  starting transfers between devices  18.5 us (17%)
  waiting for transfers between devices  14.5 us (13%)
  other arithmetic  4.47 us (4%)
  local copies, waits for them, and re-layouts  1.3 us (1%)
    all_to_all x1, blocking collectives, exchange(): lax.all_to_all(value.reshape(groups, rows // groups, tokens), 'ctx', spli...  31.8 us
    all_to_all x2, waiting for transfers between devices, exchange(): lax.all_to_all(value.reshape(groups, rows // groups, tokens), 'ctx', spli...  12.2 us
    all_to_all x2, starting transfers between devices, exchange(): lax.all_to_all(value.reshape(groups, rows // groups, tokens), 'ctx', spli...  11.3 us
    pallas_call x2, Pallas kernels, project_other(): pl.pallas_call(other_kernel, grid_spec=pltpu.PrefetchScalarGridSpec(num_s...  11.1 us
    pallas_call x1, Pallas kernels, response_call(): pl.pallas_call(response_kernel, grid=(rows // block,), in_specs=[pl.Block...  7.93 us
    pallas_call x2, Pallas kernels, short_conv(): pl.pallas_call(body, grid=(rows // block,), in_specs=specs + table_specs,...  7.44 us
    pallas_call x1, Pallas kernels, convolve_call(): pl.pallas_call(functools.partial(convolve_kernel, block), in_specs=[here,...  6.5 us
    pallas_call x1, Pallas kernels, project_own(): pl.pallas_call(own_kernel, grid_spec=pltpu.PrefetchScalarGridSpec(num_sca...  4.74 us
  transfers between devices with their start and end apart: 5, of which 3 were waited for; matrix products, arithmetic and copies ran while one was open for 3% of the time, Pallas kernels for 25%

profile of v3, /device:TPU:1, one launch (start us, length us, event | category | flops | bytes accessed | tf_op | source)
XLA Modules:
  0.0 108.5 jit_solution(4672157450391948707)
XLA Ops:
  0.0 0.0 copy-start.10
  0.0 4.5 %shard_map.181 = (bf16[2048,128]{1,0:T(8,128)(2,1)}, bf16[2048,128]{1,0:T(8,128)(2,1)}) custom-call(bf16[2048,256]{1,0:T(8,128)(2,1)} %key.5, bf16[2048,256]{1,0:T(8,128)(2,1)} %value.3, bf16[2048,256]{1,0:T(8,128)(2,1)} %query.3, f32[2048,128]{1,0:T(8,128)} %taps.3, bf16[256,256]{1,0:T(8,128)(2,1)} %constant.26.clone.fwd_hi, ...), custom_call_target="tpu_custom_call" | custom-call | flops 6710886400 | bytes 4194304 | tf_op jit(solution)/shard_map/pallas_call | solution.py:102
  4.6 4.7 %collective-permute-start = (bf16[2048,128]{1,0:T(8,128)(2,1)}, bf16[2048,128]{1,0:T(8,128)(2,1)}, u32[]{:S(2)}, u32[]{:S(2)}) collective-permute-start(bf16[2048,128]{1,0:T(8,128)(2,1)} %get-tuple-element.13), channel_id=1, source_target_pairs={{0,2},{2,4},{4,6},{6,8},{8,10},{10,12},{12,14},{14,16},{16,18},{18... | collective-permute-start | bytes 1572872 | tf_op jit(solution)/shard_map/ppermute | solution.py:483
  9.2 1.3 %collective-permute-start.2 = (bf16[2048,128]{1,0:T(8,128)(2,1)}, bf16[2048,128]{1,0:T(8,128)(2,1)}, u32[]{:S(2)}, u32[]{:S(2)}) collective-permute-start(bf16[2048,128]{1,0:T(8,128)(2,1)} %get-tuple-element.15.late), channel_id=1, source_target_pairs={{0,1},{1,0},{2,3},{3,2},{4,5},{5,4},{6,7},{7,6},{8,9},{9,8},{10,11... | collective-permute-start | bytes 1572872 | tf_op jit(solution)/shard_map/ppermute | solution.py:484
  10.5 5.0 %all-to-all-start.1 = ((bf16[16,128,256]{2,1,0:T(8,128)(2,1)}), bf16[16,128,256]{2,1,0:T(8,128)(2,1)}, u32[]{:S(2)}, u32[]{:S(2)}) async-start(bf16[16,128,256]{2,1,0:T(8,128)(2,1)} %bitcast.6), calls=%async_computation.1 | async-start | bytes 2097152 | tf_op jit(solution)/shard_map/all_to_all | solution.py:466
  15.5 0.1 collective-permute-done.border
  15.7 1.2 %copy-done.4 = f32[2048,128]{1,0:T(8,128)S(1)} copy-done((f32[2048,128]{1,0:T(8,128)S(1)}, f32[2048,128]{1,0:T(8,128)}, u32[]{:S(2)}) %copy-start.4) | copy-done | bytes 1048600
  16.9 2.9 %shard_map.182.early = bf16[2048,128]{1,0:T(8,128)(2,1)S(1)} custom-call(bf16[2048,128]{1,0:T(8,128)(2,1)} %collective-permute-done.border, bf16[2048,256]{1,0:T(8,128)(2,1)S(1)} %copy-done.1, bf16[2048,256]{1,0:T(8,128)(2,1)S(1)} %copy-done.2, bf16[2048,256]{1,0:T(8,128)(2,1)S(1)} %copy-done.3, f32[2048,128]{1,0:T(8,128)S(1)} %copy-done.4, ...), custom_call_target="tpu_custom_call" | custom-call | flops 6710886400 | bytes 4194304 | tf_op jit(solution)/shard_map/pallas_call | solution.py:102
  19.8 0.0 copy-start.5
  19.9 1.3 %collective-permute-start.1 = (bf16[2048,128]{1,0:T(8,128)(2,1)S(1)}, bf16[2048,128]{1,0:T(8,128)(2,1)S(1)}, u32[]{:S(2)}, u32[]{:S(2)}) collective-permute-start(bf16[2048,128]{1,0:T(8,128)(2,1)S(1)} %shard_map.182.early), channel_id=1, source_target_pairs={{0,1},{1,0},{2,3},{3,2},{4,5},{5,4},{6,7},{7,6},{8,9},{9,8},{10,11... | collective-permute-start | bytes 1572872 | tf_op jit(solution)/shard_map/ppermute | solution.py:488
  21.1 4.7 %shard_map.183 = (f32[2048,128]{1,0:T(8,128)S(1)}, f32[2048,128]{1,0:T(8,128)S(1)}) custom-call(s32[1]{0:T(128)} %bitcast.which, bf16[2048,4096]{1,0:T(8,128)(2,1)} %weight.5, bf16[2048,128]{1,0:T(8,128)(2,1)S(1)} %copy-done, bf16[2048,128]{1,0:T(8,128)(2,1)S(1)} %shard_map.182.early), custom_call_target="tpu_custom_call" | custom-call | flops 2147483648 | bytes 8388608 | tf_op jit(solution)/shard_map/pallas_call | solution.py:137
  25.9 5.6 %shard_map.184.refs_0_ = bf16[2048,256]{1,0:T(8,128)(2,1)} custom-call(s32[1]{0:T(128)S(6)} %sub.4.which, bf16[2048,4096]{1,0:T(8,128)(2,1)} %weight.5, bf16[2048,128]{1,0:T(8,128)(2,1)} %collective-permute-done.2.piece, f32[2048,128]{1,0:T(8,128)S(1)} %get-tuple-element.17.total, bf16[2048,256]{1,0:T(8,128)(2,1)S(1)} %copy-done.5), custom_call_target="tpu_custom_call" | custom-call | flops 8589934592 | bytes 8388608 | tf_op jit(solution)/shard_map/pallas_call | solution.py:170
  31.5 2.2 %collective-permute-done.1.piece = bf16[2048,128]{1,0:T(8,128)(2,1)S(1)} collective-permute-done((bf16[2048,128]{1,0:T(8,128)(2,1)S(1)}, bf16[2048,128]{1,0:T(8,128)(2,1)S(1)}, u32[]{:S(2)}, u32[]{:S(2)}) %collective-permute-start.1) | collective-permute-done | bytes 524320 | tf_op jit(solution)/shard_map/ppermute | solution.py:488
  33.7 5.4 %shard_map.185 = bf16[2048,256]{1,0:T(8,128)(2,1)} custom-call(s32[1]{0:T(128)S(6)} %sub.4.which, bf16[2048,4096]{1,0:T(8,128)(2,1)} %weight.5, bf16[2048,128]{1,0:T(8,128)(2,1)S(1)} %collective-permute-done.1.piece, f32[2048,128]{1,0:T(8,128)S(1)} %get-tuple-element.16.total, bf16[2048,256]{1,0:T(8,128)(2,1)S(1)} %copy-done.5, ...), custom_call_target="tpu_custom_call", output_to_operand_aliasing={{}: (5, {})} | custom-call | flops 8589934592 | bytes 8388608 | tf_op jit(solution)/shard_map/pallas_call | solution.py:170
  39.2 6.3 %all-to-all-start = ((bf16[16,128,256]{2,1,0:T(8,128)(2,1)}), bf16[16,128,256]{2,1,0:T(8,128)(2,1)S(1)}, u32[]{:S(2)}, u32[]{:S(2)}) async-start(bf16[16,128,256]{2,1,0:T(8,128)(2,1)} %bitcast.1), calls=%async_computation | async-start | bytes 2097152 | tf_op jit(solution)/shard_map/all_to_all | solution.py:466
  45.5 3.0 %convert_multiply_fusion = f32[2048,256]{1,0:T(8,128)} fusion(bf16[2048,256]{1,0:T(8,128)(2,1)} %shard_map.185, f32[2048]{0:T(1024)S(1)} %copy-done.17), kind=kLoop, calls=%fused_computation.3 | loop fusion | flops 1048576 | bytes 3153920 | tf_op jit(solution)/shard_map/mul | solution.py:494
  48.4 0.0 copy-start.13
  48.4 0.0 copy-start.14
  48.5 7.9 %shard_map.186.response = f32[17,128,512]{2,1,0:T(8,128)} custom-call(bf16[16,128,256]{2,1,0:T(8,128)(2,1)} %all-to-all-done.1.source, f32[17,256]{1,0:T(8,128)} %constant.29.clone.turn_re, f32[17,256]{1,0:T(8,128)} %constant.30.clone.turn_im, bf16[512,512]{1,0:T(8,128)(2,1)} %constant.31.clone.high.forward, bf16[512,512]{1,0:T(8,128)(2,1)} %constant.32.clone.low), custom_call_target="tpu_custom_call" | custom-call | flops 3422552064 | bytes 128 | tf_op jit(solution)/shard_map/pallas_call | solution.py:449
  56.4 12.2 %all-to-all-done.source = bf16[16,128,256]{2,1,0:T(8,128)(2,1)S(1)} async-done(((bf16[16,128,256]{2,1,0:T(8,128)(2,1)}), bf16[16,128,256]{2,1,0:T(8,128)(2,1)S(1)}, u32[]{:S(2)}, u32[]{:S(2)}) %all-to-all-start) | async-done | bytes 1048608 | tf_op jit(solution)/shard_map/all_to_all | solution.py:466
  68.6 0.0 copy-start.16
  68.6 6.5 %shard_map.187 = bf16[16,128,256]{2,1,0:T(8,128)(2,1)S(1)} custom-call(bf16[16,128,256]{2,1,0:T(8,128)(2,1)S(1)} %all-to-all-done.source, f32[17,128,512]{2,1,0:T(8,128)} %shard_map.186.response, f32[17,256]{1,0:T(8,128)S(1)} %copy-done.12, f32[17,256]{1,0:T(8,128)S(1)} %copy-done.11, f32[17,256]{1,0:T(8,128)S(1)} %copy-done.14, f32[17,256]{1,0:T(8,128)S(1)} %copy-done.13, ...), custom_call_target="tpu_custom_call" | custom-call | flops 2281701376 | bytes 128 | tf_op jit(solution)/shard_map/pallas_call | solution.py:425
  75.2 31.8 %all_to_all.15 = bf16[16,128,256]{2,1,0:T(8,128)(2,1)S(1)} all-to-all(bf16[16,128,256]{2,1,0:T(8,128)(2,1)S(1)} %shard_map.187), channel_id=1, replica_groups=mesh['ctx'=16,'ch'=2] {'ctx'}, dimensions={0} | all-to-all | bytes 2097152 | tf_op jit(solution)/shard_map/all_to_all | solution.py:466
  107.0 1.5 %fusion.1 = bf16[2048,256]{1,0:T(8,128)(2,1)} fusion(f32[2048,256]{1,0:T(8,128)S(1)} %copy-done.15, bf16[2048,256]{1,0:T(8,128)(2,1)S(1)} %copy-done.16, bf16[16,128,256]{2,1,0:T(8,128)(2,1)S(1)} %all_to_all.15), kind=kLoop, calls=%fused_computation.2 | loop fusion | flops 2621440 | bytes 5242880 | tf_op jit(solution)/shard_map/convert_element_type | solution.py:499
  (32 shorter events, 0.1 us)
Async XLA Ops:
  0.0 15.7 %copy-start.3 = (bf16[2048,256]{1,0:T(8,128)(2,1)S(1)}, bf16[2048,256]{1,0:T(8,128)(2,1)}, u32[]{:S(2)}) copy-start(bf16[2048,256]{1,0:T(8,128)(2,1)} %query.3) | copy-start | bytes 3145732
  0.0 15.7 %copy-start.8 = (bf16[256,256]{1,0:T(8,128)(2,1)S(1)}, bf16[256,256]{1,0:T(8,128)(2,1)}, u32[]{:S(2)}) copy-start(bf16[256,256]{1,0:T(8,128)(2,1)} %constant.28.clone.inverse) | copy-start | bytes 393220
  0.0 15.7 %copy-start.9 = (bf16[256,256]{1,0:T(8,128)(2,1)S(1)}, bf16[256,256]{1,0:T(8,128)(2,1)}, u32[]{:S(2)}) copy-start(bf16[256,256]{1,0:T(8,128)(2,1)} %constant.27.clone.fwd_lo) | copy-start | bytes 393220
  0.0 15.7 %copy-start.10 = (bf16[256,256]{1,0:T(8,128)(2,1)S(1)}, bf16[256,256]{1,0:T(8,128)(2,1)}, u32[]{:S(2)}) copy-start(bf16[256,256]{1,0:T(8,128)(2,1)} %constant.26.clone.fwd_hi) | copy-start | bytes 393220
  4.5 11.1 %copy-start.1 = (bf16[2048,256]{1,0:T(8,128)(2,1)S(1)}, bf16[2048,256]{1,0:T(8,128)(2,1)}, u32[]{:S(2)}) copy-start(bf16[2048,256]{1,0:T(8,128)(2,1)} %key.5) | copy-start | bytes 3145732
  4.5 11.1 %copy-start.2 = (bf16[2048,256]{1,0:T(8,128)(2,1)S(1)}, bf16[2048,256]{1,0:T(8,128)(2,1)}, u32[]{:S(2)}) copy-start(bf16[2048,256]{1,0:T(8,128)(2,1)} %value.3) | copy-start | bytes 3145732
  4.6 11.1 %collective-permute-start = (bf16[2048,128]{1,0:T(8,128)(2,1)}, bf16[2048,128]{1,0:T(8,128)(2,1)}, u32[]{:S(2)}, u32[]{:S(2)}) collective-permute-start(bf16[2048,128]{1,0:T(8,128)(2,1)} %get-tuple-element.13), channel_id=1, source_target_pairs={{0,2},{2,4},{4,6},{6,8},{8,10},{10,12},{12,14},{14,16},{16,18},{18... | collective-permute-start | bytes 1572872 | tf_op jit(solution)/shard_map/ppermute | solution.py:483
  9.2 16.6 %collective-permute-start.2 = (bf16[2048,128]{1,0:T(8,128)(2,1)}, bf16[2048,128]{1,0:T(8,128)(2,1)}, u32[]{:S(2)}, u32[]{:S(2)}) collective-permute-start(bf16[2048,128]{1,0:T(8,128)(2,1)} %get-tuple-element.15.late), channel_id=1, source_target_pairs={{0,1},{1,0},{2,3},{3,2},{4,5},{5,4},{6,7},{7,6},{8,9},{9,8},{10,11... | collective-permute-start | bytes 1572872 | tf_op jit(solution)/shard_map/ppermute | solution.py:484
  10.5 28.6 %all-to-all-start.1 = ((bf16[16,128,256]{2,1,0:T(8,128)(2,1)}), bf16[16,128,256]{2,1,0:T(8,128)(2,1)}, u32[]{:S(2)}, u32[]{:S(2)}) async-start(bf16[16,128,256]{2,1,0:T(8,128)(2,1)} %bitcast.6), calls=%async_computation.1 | async-start | bytes 2097152 | tf_op jit(solution)/shard_map/all_to_all | solution.py:466
  15.5 5.6 %copy-start = (bf16[2048,128]{1,0:T(8,128)(2,1)S(1)}, bf16[2048,128]{1,0:T(8,128)(2,1)}, u32[]{:S(2)}) copy-start(bf16[2048,128]{1,0:T(8,128)(2,1)} %get-tuple-element.15.late) | copy-start | bytes 1572868
  15.7 1.2 %copy-start.4 = (f32[2048,128]{1,0:T(8,128)S(1)}, f32[2048,128]{1,0:T(8,128)}, u32[]{:S(2)}) copy-start(f32[2048,128]{1,0:T(8,128)} %taps.3) | copy-start | bytes 3145732
  19.8 6.0 %copy-start.5 = (bf16[2048,256]{1,0:T(8,128)(2,1)S(1)}, bf16[2048,256]{1,0:T(8,128)(2,1)}, u32[]{:S(2)}) copy-start(bf16[2048,256]{1,0:T(8,128)(2,1)} %key.7) | copy-start | bytes 3145732
  19.9 13.8 %collective-permute-start.1 = (bf16[2048,128]{1,0:T(8,128)(2,1)S(1)}, bf16[2048,128]{1,0:T(8,128)(2,1)S(1)}, u32[]{:S(2)}, u32[]{:S(2)}) collective-permute-start(bf16[2048,128]{1,0:T(8,128)(2,1)S(1)} %shard_map.182.early), channel_id=1, source_target_pairs={{0,1},{1,0},{2,3},{3,2},{4,5},{5,4},{6,7},{7,6},{8,9},{9,8},{10,11... | collective-permute-start | bytes 1572872 | tf_op jit(solution)/shard_map/ppermute | solution.py:488
  39.1 6.3 %copy-start.17 = (f32[2048]{0:T(1024)S(1)}, f32[2048]{0:T(1024)}, u32[]{:S(2)}) copy-start(f32[2048]{0:T(1024)} %param.27) | copy-start | bytes 24580
  39.2 29.4 %all-to-all-start = ((bf16[16,128,256]{2,1,0:T(8,128)(2,1)}), bf16[16,128,256]{2,1,0:T(8,128)(2,1)S(1)}, u32[]{:S(2)}, u32[]{:S(2)}) async-start(bf16[16,128,256]{2,1,0:T(8,128)(2,1)} %bitcast.1), calls=%async_computation | async-start | bytes 2097152 | tf_op jit(solution)/shard_map/all_to_all | solution.py:466
  48.4 20.2 %copy-start.6 = (bf16[512,512]{1,0:T(8,128)(2,1)S(1)}, bf16[512,512]{1,0:T(8,128)(2,1)}, u32[]{:S(2)}) copy-start(bf16[512,512]{1,0:T(8,128)(2,1)} %constant.31.clone.high.forward) | copy-start | bytes 1572868
  48.4 20.2 %copy-start.7 = (bf16[512,512]{1,0:T(8,128)(2,1)S(1)}, bf16[512,512]{1,0:T(8,128)(2,1)}, u32[]{:S(2)}) copy-start(bf16[512,512]{1,0:T(8,128)(2,1)} %constant.35.clone.inverse) | copy-start | bytes 1572868
  48.4 20.2 %copy-start.11 = (f32[17,256]{1,0:T(8,128)S(1)}, f32[17,256]{1,0:T(8,128)}, u32[]{:S(2)}) copy-start(f32[17,256]{1,0:T(8,128)} %constant.30.clone.turn_im) | copy-start | bytes 52228
  48.4 20.2 %copy-start.12 = (f32[17,256]{1,0:T(8,128)S(1)}, f32[17,256]{1,0:T(8,128)}, u32[]{:S(2)}) copy-start(f32[17,256]{1,0:T(8,128)} %constant.29.clone.turn_re) | copy-start | bytes 52228
  48.4 20.2 %copy-start.13 = (f32[17,256]{1,0:T(8,128)S(1)}, f32[17,256]{1,0:T(8,128)}, u32[]{:S(2)}) copy-start(f32[17,256]{1,0:T(8,128)} %constant.34.clone.back_im) | copy-start | bytes 52228
  48.4 20.2 %copy-start.14 = (f32[17,256]{1,0:T(8,128)S(1)}, f32[17,256]{1,0:T(8,128)}, u32[]{:S(2)}) copy-start(f32[17,256]{1,0:T(8,128)} %constant.33.clone.back_re) | copy-start | bytes 52228
  68.6 38.3 %copy-start.16 = (bf16[2048,256]{1,0:T(8,128)(2,1)S(1)}, bf16[2048,256]{1,0:T(8,128)(2,1)}, u32[]{:S(2)}) copy-start(bf16[2048,256]{1,0:T(8,128)(2,1)} %param.24) | copy-start | bytes 3145732
  75.1 31.8 %copy-start.15 = (f32[2048,256]{1,0:T(8,128)S(1)}, f32[2048,256]{1,0:T(8,128)}, u32[]{:S(2)}) copy-start(f32[2048,256]{1,0:T(8,128)} %convert_multiply_fusion) | copy-start | bytes 6291460
